TPU v7x, 512 devices: a whole 4x8x8 slice. The times are simulated.
512 devices in a mesh: img: 16 (over y, core), proj: 32 (over z, x).
Axes of the slice: x: 4, y: 8, z: 8, core: 2. Of those that a mesh axis runs over, the one named last changes fastest.
Arguments:
- images: bfloat16 [2048, 4096], P('img'), may hold values from -48 to 48
- projections: bfloat16 [2560, 4096], P('proj'), may hold values from -6 to 6
- noise_weight: float32 [4096], replicated, may hold values from 0.02 to 0.08
- defocus: float32 [2048], P('img'), may hold values from 2 to 8
- orient_count: int32 [2048], P('img'), may hold values from 160 to 2560, as said below
- term_limit: int32 [2048], P('img'), may hold values from 2048 to 4096
- block_plan: int32 [64], replicated, may hold values from 0 to 63, each once
Outputs:
- reconstruction: bfloat16 [2560, 4096], P('proj', 'img')
- evidence_next: float32 [2048], P('img')
Inputs may be any that keep to these rules, and one draw needn't show every extreme that they name: Orientations 0 to orient_count[i] - 1 are the significant ones of image i; some image has all 2560.
All inputs are finite; a program needn't handle non-finite values.
Results may differ from a plain program's by a relative error of at most 0.018.
Values may be sent and summed in bfloat16 or wider, within the bound.
No kernel may reach another device: no remote copies, remote signals or barrier semaphores. Data moves between devices by JAX's collectives and lax.ppermute only.
A program may use at most 64 MiB of HBM per device.

v0:
```python
import functools
import math

import jax
import jax.numpy as jnp
from jax import lax
from jax.experimental import pallas as pl
from jax.experimental.pallas import tpu as pltpu
from jax.sharding import PartitionSpec as P

F = 4096
BLOCK = 32
LANES = 128
COLS = 256
PAD = 8
PARTS = 8
BF = jnp.bfloat16
F32 = jnp.float32


def small_sin_cos(x):
    y = x * x
    s = 1.0
    for k in (12, 10, 8, 6, 4, 2):
        s = 1.0 - y * s * (1.0 / (k * (k + 1)))
    c = 1.0
    for k in (14, 12, 10, 8, 6, 4, 2):
        c = 1.0 - y * c * (1.0 / (k * (k - 1)))
    return x * s, c


def down_rows(row):
    n = row.shape[1]
    return jnp.transpose(jnp.broadcast_to(row, (n, n)))


def set_turn(defocus, limits, turn, edge):
    images = turn.shape[1]
    lane = lax.broadcasted_iota(jnp.int32, (images, LANES), 1).astype(F32)
    angle = down_rows(defocus) * ((lane + 1.0) * (2.0 * math.pi / F))
    base_s, base_c = small_sin_cos(angle)
    first_s = base_s * math.cos(0.1) + base_c * math.sin(0.1)
    first_c = base_c * math.cos(0.1) - base_s * math.sin(0.1)
    step_s = jnp.broadcast_to(base_s[:, LANES - 1 :], (images, LANES))
    step_c = jnp.broadcast_to(base_c[:, LANES - 1 :], (images, LANES))
    turn[0] = first_s
    turn[1] = first_s * step_c - first_c * step_s
    turn[2] = step_c + step_c
    edge[...] = down_rows(limits.astype(F32)) - lane


def walk(g, pixels, turn, edge, use):
    for r in range(0, pixels.shape[0], 16):
        some = slice(r, r + 16)
        s, before = turn[0, some], turn[1, some]
        twice = turn[2, some]
        last = edge[some]
        for h in range(COLS // LANES):
            first = g * COLS + h * LANES
            at = slice(first, first + LANES)
            kept = jnp.where(last > float(first), s, 0.0)
            use(some, at, slice(h * LANES, (h + 1) * LANES), kept * pixels[some, at].astype(F32), kept * s)
            s, before = twice * s - before, s
        turn[0, some], turn[1, some] = s, before


def score_kernel(
    far_pixels, far_proj, far_noise, far_defocus, far_counts, far_limits, scores, stats,
    pixels, proj, noise, defocus, counts, limits, terms, terms_sq, turn, edge, arrived, small_arrived,
):
    rows, images = proj.shape[0], pixels.shape[0]
    small = [
        pltpu.make_async_copy(far, near, small_arrived.at[k])
        for k, (far, near) in enumerate(
            ((far_defocus, defocus), (far_limits, limits), (far_noise, noise), (far_counts, counts))
        )
    ]
    for copy in small:
        copy.start()
    copies = []
    for n in range(PARTS):
        at = pl.ds(n * (F // PARTS), F // PARTS)
        copies.append(
            [
                pltpu.make_async_copy(far.at[:, at], near.at[:, at], arrived.at[k, n])
                for k, (far, near) in enumerate(((far_pixels, pixels), (far_proj, proj)))
            ]
        )
        for copy in copies[-1]:
            copy.start()
    for copy in small:
        copy.wait()
    set_turn(defocus[...], limits[...], turn, edge)

    def use(some, at, inner, image, square):
        weight = noise[:, at]
        terms[some, at] = (weight * image).astype(BF)
        terms_sq[some, at] = ((-0.5 * weight) * square).astype(BF)

    total = jnp.zeros((rows, images), F32)
    contract = (((1,), (1,)), ((), ()))
    groups = F // COLS
    for g in range(groups):
        if g % (groups // PARTS) == 0:
            for copy in copies[g // (groups // PARTS)]:
                copy.wait()
        walk(g, pixels, turn, edge, use)
        at = slice(g * COLS, (g + 1) * COLS)
        some_proj = proj[:, at]
        wide = some_proj.astype(F32)
        total += lax.dot_general(some_proj, terms[:, at], contract, preferred_element_type=F32)
        total += lax.dot_general((wide * wide).astype(BF), terms_sq[:, at], contract, preferred_element_type=F32)
    orient = lax.axis_index("proj") * rows + lax.broadcasted_iota(jnp.int32, (rows, images), 0)
    significant = orient < counts[...]
    found = jnp.where(significant, total, -1e30)
    peak = jnp.max(found, axis=0, keepdims=True)
    mass = jnp.sum(jnp.where(significant, jnp.exp(found - peak), 0.0), axis=0, keepdims=True)
    scores[...] = found
    both = jnp.concatenate([peak, mass], axis=0)
    stats[...] = jnp.broadcast_to(both[None], stats.shape)


def terms_kernel(far_pixels, defocus, limits, plan, back, chosen, pixels, turn, edge, arrived):
    copy = pltpu.make_async_copy(far_pixels, pixels, arrived)
    copy.start()
    set_turn(defocus[...], limits[...], turn, edge)
    copy.wait()
    for g in range(F // COLS):

        def use(some, at, inner, image, square):
            back[g, 0, some, inner] = image.astype(BF)
            back[g, 1, some, inner] = square.astype(BF)

        walk(g, pixels, turn, edge, use)
    per_line = LANES // BLOCK
    shape = chosen.shape[1:]
    blocks = plan.shape[1]
    line = lax.broadcasted_iota(jnp.int32, (shape[0], blocks), 0)
    number = lax.broadcasted_iota(jnp.int32, (shape[0], blocks), 1)
    group = lax.broadcasted_iota(jnp.int32, shape, 1) // BLOCK
    goal = jnp.broadcast_to(plan[...], (shape[0], blocks)).astype(F32)
    target = jnp.zeros(shape, F32)
    for k in range(per_line):
        mine = jnp.sum(jnp.where(number == line * per_line + k, goal, 0.0), axis=1, keepdims=True)
        target = jnp.where(group == k, mine, target)
    slot = (lax.axis_index("img") * per_line + group).astype(F32)
    for k in range(per_line):
        moved = target if k == 0 else pltpu.roll(target, k * BLOCK, 1)
        chosen[k] = jnp.where(moved == slot, 1.0, 0.0)


def thirds(x):
    first = x.astype(BF)
    rest = x - first.astype(F32)
    second = rest.astype(BF)
    return first, second, (rest - second.astype(F32)).astype(BF)


def back_kernel(scores, stats, back, counts, own, other):
    rows, images = scores.shape
    peaks, masses = stats[:, 0, :], stats[:, 1, :]
    peak = jnp.max(peaks, axis=0, keepdims=True)
    mass = jnp.sum(masses * jnp.exp(peaks - peak), axis=0, keepdims=True)
    evidence = peak + jnp.log(mass)
    orient = lax.axis_index("proj") * rows + lax.broadcasted_iota(jnp.int32, (rows, images), 0)
    significant = orient < counts[...]
    posterior = jnp.where(significant, jnp.exp(scores[...] - evidence), 0.0).astype(BF)
    core = lax.rem(lax.axis_index("img"), 2)
    here = lax.broadcasted_iota(jnp.int32, (PAD, COLS), 1) // LANES == core
    line = lax.broadcasted_iota(jnp.int32, (PAD, COLS), 0)
    wide = jnp.concatenate([evidence, evidence], axis=1)
    note = jnp.zeros((PAD, COLS), F32)
    for k, part in enumerate(thirds(wide)):
        note = jnp.where(line == k, part.astype(F32), note)
    note = jnp.where(here, note, 0.0).astype(BF)
    for out, side in ((own, core), (other, 1 - core)):
        for y in range(own.shape[0]):
            for k in range(2):
                part = jnp.dot(posterior, back[2 * y + side, k], preferred_element_type=F32)
                out[y, k * rows : (k + 1) * rows, :] = part.astype(BF)
            out[y, 2 * rows :, :] = note


def last_kernel(parts, chosen, far_reconstruction, far_evidence, reconstruction, evidence, sent):
    rows = reconstruction.shape[0]
    chips = parts.shape[0]
    images = parts[0, :rows, :].astype(F32)
    weights = parts[0, rows : 2 * rows, :].astype(F32)
    for y in range(1, chips):
        images += parts[y, :rows, :].astype(F32)
        weights += parts[y, rows : 2 * rows, :].astype(F32)
    reconstruction[...] = (images / (weights + 1.0)).astype(BF)
    first = pltpu.make_async_copy(reconstruction, far_reconstruction, sent.at[0])
    first.start()
    lines = []
    for y in range(chips):
        note = parts[y, 2 * rows :, :].astype(F32)
        full = (note[0:1] + note[1:2]) + note[2:3]
        lines += [full[:, :LANES], full[:, LANES:]]
    known = jnp.concatenate(lines, axis=0)
    placed = jnp.zeros((1, LANES), F32)
    for k in range(LANES // BLOCK):
        moved = known if k == 0 else pltpu.roll(known, k * BLOCK, 1)
        placed += jnp.sum(jnp.where(chosen[k] > 0.0, moved, 0.0), axis=0, keepdims=True)
    evidence[...] = placed
    second = pltpu.make_async_copy(evidence, far_evidence, sent.at[1])
    second.start()
    first.wait()
    second.wait()


def kept_far(array):
    return pltpu.with_memory_space_constraint(array, pltpu.HBM)


def vmem(n):
    return [pl.BlockSpec(memory_space=pltpu.VMEM)] * n


def shards(images, projections, noise_weight, defocus, orient_count, term_limit, block_plan):
    rows, count = projections.shape[0], images.shape[0]
    devices, peers = lax.axis_size("img"), lax.axis_size("proj")
    chips = devices // 2
    limit = pltpu.CompilerParams(vmem_limit_bytes=48 * 2**20)
    counts = orient_count.reshape(1, count)
    focus, limits = defocus.reshape(1, count), term_limit.reshape(1, count)
    tables = [pltpu.VMEM((3, count, LANES), F32), pltpu.VMEM((count, LANES), F32)]
    scores, stats = pl.pallas_call(
        score_kernel,
        name="score",
        out_shape=(
            jax.ShapeDtypeStruct((rows, count), F32),
            jax.ShapeDtypeStruct((peers, 2, count), F32),
        ),
        in_specs=[pl.BlockSpec(memory_space=pltpu.HBM)] * 6,
        out_specs=tuple(vmem(2)),
        scratch_shapes=[
            pltpu.VMEM((count, F), BF),
            pltpu.VMEM((rows, F), BF),
            pltpu.VMEM((1, F), F32),
            pltpu.VMEM((1, count), F32),
            pltpu.VMEM((1, count), jnp.int32),
            pltpu.VMEM((1, count), jnp.int32),
            pltpu.VMEM((count, F), BF),
            pltpu.VMEM((count, F), BF),
            *tables,
            pltpu.SemaphoreType.DMA((2, PARTS)),
            pltpu.SemaphoreType.DMA((4,)),
        ],
        compiler_params=limit,
    )(*map(kept_far, (images, projections, noise_weight.reshape(1, F), focus, counts, limits)))
    back, chosen = pl.pallas_call(
        terms_kernel,
        name="terms",
        out_shape=(
            jax.ShapeDtypeStruct((devices, 2, count, COLS), BF),
            jax.ShapeDtypeStruct((LANES // BLOCK, devices, LANES), F32),
        ),
        in_specs=[pl.BlockSpec(memory_space=pltpu.HBM), *vmem(3)],
        out_specs=tuple(vmem(2)),
        scratch_shapes=[pltpu.VMEM((count, F), BF), *tables, pltpu.SemaphoreType.DMA],
        compiler_params=limit,
        cost_estimate=pl.CostEstimate(flops=20 * count * F, bytes_accessed=6 * count * F, transcendentals=0),
    )(kept_far(images), focus, limits, block_plan.reshape(1, -1))
    stats = lax.all_to_all(stats, "proj", 0, 0, tiled=True)
    shape = jax.ShapeDtypeStruct((chips, 2 * rows + PAD, COLS), BF)
    own, other = pl.pallas_call(
        back_kernel,
        name="back",
        out_shape=(shape, shape),
        in_specs=vmem(4),
        out_specs=tuple(vmem(2)),
        compiler_params=limit,
    )(scores, stats, back, counts)
    other = lax.ppermute(other, "img", [(i, i ^ 1) for i in range(devices)])
    both = (own.astype(F32) + other.astype(F32)).astype(BF)
    same_core = [[2 * y + c for y in range(chips)] for c in range(2)]
    parts = lax.all_to_all(both, "img", 0, 0, tiled=True, axis_index_groups=same_core)
    reconstruction, evidence = pl.pallas_call(
        last_kernel,
        name="last",
        out_shape=(
            jax.ShapeDtypeStruct((rows, COLS), BF),
            jax.ShapeDtypeStruct((1, count), F32),
        ),
        in_specs=vmem(2),
        out_specs=tuple([pl.BlockSpec(memory_space=pltpu.HBM)] * 2),
        scratch_shapes=[
            pltpu.VMEM((rows, COLS), BF),
            pltpu.VMEM((1, count), F32),
            pltpu.SemaphoreType.DMA((2,)),
        ],
        compiler_params=limit,
    )(parts, chosen)
    return reconstruction, evidence.reshape(count)


def solution(mesh):
    placed = (P("img", None), P("proj", None), P(), P("img"), P("img"), P("img"), P())
    return jax.shard_map(
        shards, mesh=mesh, in_specs=placed, out_specs=(P("proj", "img"), P("img")), check_vma=False
    )
```

profile of v0, /device:TPU:1, one launch (start us, length us, event | category | flops | bytes accessed | tf_op | source)
XLA Modules:
  0.0 61.5 jit_solution(10639570917325258035)
XLA Ops:
  0.6 0.0 copy-start.1
  0.6 0.0 copy-start
  0.7 0.0 copy-start.3
  0.7 0.0 copy-start.2
  0.7 4.3 %score.1 = (f32[80,128]{1,0:T(8,128)S(1)}, f32[32,2,128]{2,1,0:T(2,128)}) custom-call(bf16[128,4096]{1,0:T(8,128)(2,1)} %far_pixels.3, bf16[80,4096]{1,0:T(8,128)(2,1)} %far_proj.1, f32[1,4096]{1,0:T(1,128)} %bitcast.13, f32[1,128]{1,0:T(1,128)} %bitcast.6, s32[1,128]{1,0:T(1,128)} %bitcast.10, s32[1,128]{1,0:T(1,128)} %bitcast.8), custom_call_target="tpu_custom_call" | custom-call | tf_op jit(solution)/shard_map/score/pallas_call | solution.py:228
  4.9 13.7 %all-to-all-start = ((f32[32,2,128]{2,1,0:T(2,128)}), f32[32,2,128]{2,1,0:T(2,128)S(1)}, u32[]{:S(2)}, u32[]{:S(2)}) async-start(f32[32,2,128]{2,1,0:T(2,128)} %get-tuple-element.11), calls=%async_computation | async-start | bytes 65536 | tf_op jit(solution)/shard_map/all_to_all | solution.py:265
  18.7 0.0 copy-done.1
  18.7 0.0 copy-done
  18.7 0.0 copy-done.3
  18.7 2.0 %terms.1 = (bf16[16,2,128,256]{3,2,1,0:T(8,128)(2,1)S(1)}, f32[4,16,128]{2,1,0:T(8,128)S(1)}) custom-call(bf16[128,4096]{1,0:T(8,128)(2,1)} %far_pixels.3, f32[1,128]{1,0:T(1,128)S(1)} %bitcast.7, s32[1,128]{1,0:T(1,128)S(1)} %bitcast.9, s32[1,64]{1,0:T(1,128)S(1)} %bitcast.12), custom_call_target="tpu_custom_call" | custom-call | flops 10485760 | bytes 3145728 | tf_op jit(solution)/shard_map/terms/pallas_call | solution.py:252
  20.8 6.6 %all-to-all-done.stats = f32[32,2,128]{2,1,0:T(2,128)S(1)} async-done(((f32[32,2,128]{2,1,0:T(2,128)}), f32[32,2,128]{2,1,0:T(2,128)S(1)}, u32[]{:S(2)}, u32[]{:S(2)}) %all-to-all-start) | async-done | bytes 32800 | tf_op jit(solution)/shard_map/all_to_all | solution.py:265
  27.4 0.0 copy-done.2
  27.4 0.5 back.1
  27.9 4.0 %collective-permute-start = (bf16[8,168,256]{2,1,0:T(8,128)(2,1)S(1)}, bf16[8,168,256]{2,1,0:T(8,128)(2,1)S(1)}, u32[]{:S(2)}, u32[]{:S(2)}) collective-permute-start(bf16[8,168,256]{2,1,0:T(8,128)(2,1)S(1)} %get-tuple-element.14), channel_id=1, source_target_pairs={{0,32},{32,0},{64,96},{96,64},{128,160},{160,128},{192,224},{224,1... | collective-permute-start | bytes 2064392 | tf_op jit(solution)/shard_map/ppermute | solution.py:275
  31.9 1.7 %collective-permute-done = bf16[8,168,256]{2,1,0:T(8,128)(2,1)S(1)} collective-permute-done((bf16[8,168,256]{2,1,0:T(8,128)(2,1)S(1)}, bf16[8,168,256]{2,1,0:T(8,128)(2,1)S(1)}, u32[]{:S(2)}, u32[]{:S(2)}) %collective-permute-start) | collective-permute-done | bytes 688160 | tf_op jit(solution)/shard_map/ppermute | solution.py:275
  33.7 0.2 add_convert_fusion
  33.9 26.8 %all_to_all.10.parts = bf16[8,168,256]{2,1,0:T(8,128)(2,1)S(1)} all-to-all(bf16[8,168,256]{2,1,0:T(8,128)(2,1)S(1)} %add_convert_fusion), channel_id=1, replica_groups={{0,64,128,192,256,320,384,448},{32,96,160,224,288,352,416,480},{1,65,12..., dimensions={0} | all-to-all | bytes 1376256 | tf_op jit(solution)/shard_map/all_to_all | solution.py:278
  60.7 0.7 %last.1 = (bf16[80,256]{1,0:T(8,128)(2,1)}, f32[1,128]{1,0:T(1,128)}) custom-call(bf16[8,168,256]{2,1,0:T(8,128)(2,1)S(1)} %all_to_all.10.parts, f32[4,16,128]{2,1,0:T(8,128)S(1)} %get-tuple-element.15.chosen), custom_call_target="tpu_custom_call" | custom-call | tf_op jit(solution)/shard_map/last/pallas_call | solution.py:279
Async XLA Ops:
  0.6 18.0 %copy-start.1 = (s32[128]{0:T(128)S(1)}, s32[128]{0:T(128)}, u32[]{:S(2)}) copy-start(s32[128]{0:T(128)} %param.12) | copy-start | bytes 1540
  0.6 18.0 %copy-start = (f32[128]{0:T(128)S(1)}, f32[128]{0:T(128)}, u32[]{:S(2)}) copy-start(f32[128]{0:T(128)} %param.10) | copy-start | bytes 1540
  0.7 18.0 %copy-start.3 = (s32[64]{0:T(128)S(1)}, s32[64]{0:T(128)}, u32[]{:S(2)}) copy-start(s32[64]{0:T(128)} %param.13) | copy-start | bytes 772
  0.7 26.7 %copy-start.2 = (s32[128]{0:T(128)S(1)}, s32[128]{0:T(128)}, u32[]{:S(2)}) copy-start(s32[128]{0:T(128)} %param.11) | copy-start | bytes 1540
  4.9 22.4 %all-to-all-start = ((f32[32,2,128]{2,1,0:T(2,128)}), f32[32,2,128]{2,1,0:T(2,128)S(1)}, u32[]{:S(2)}, u32[]{:S(2)}) async-start(f32[32,2,128]{2,1,0:T(2,128)} %get-tuple-element.11), calls=%async_computation | async-start | bytes 65536 | tf_op jit(solution)/shard_map/all_to_all | solution.py:265
  27.9 5.8 %collective-permute-start = (bf16[8,168,256]{2,1,0:T(8,128)(2,1)S(1)}, bf16[8,168,256]{2,1,0:T(8,128)(2,1)S(1)}, u32[]{:S(2)}, u32[]{:S(2)}) collective-permute-start(bf16[8,168,256]{2,1,0:T(8,128)(2,1)S(1)} %get-tuple-element.14), channel_id=1, source_target_pairs={{0,32},{32,0},{64,96},{96,64},{128,160},{160,128},{192,224},{224,1... | collective-permute-start | bytes 2064392 | tf_op jit(solution)/shard_map/ppermute | solution.py:275
where the time goes:
time: 61.7 us; the launch traced here: 61.5 us
  blocking collectives  26.8 us (43%)
  starting transfers between devices  17.7 us (29%)
  waiting for transfers between devices  8.36 us (14%)
  Pallas kernels  7.59 us (12%)
  between operations  0.73 us (1%)
    all_to_all x1, blocking collectives, shards(): lax.all_to_all(both, 'img', 0, 0, tiled=True, axis_index_groups=same_core)  26.8 us
    all_to_all x1, starting transfers between devices, shards(): stats = lax.all_to_all(stats, 'proj', 0, 0, tiled=True)  13.7 us
    all_to_all x1, waiting for transfers between devices, shards(): stats = lax.all_to_all(stats, 'proj', 0, 0, tiled=True)  6.61 us
    pallas_call x1, Pallas kernels, shards(): pl.pallas_call(score_kernel, name='score', out_shape=(jax.ShapeDtypeStruc...  4.26 us
    ppermute x1, starting transfers between devices, shards(): other = lax.ppermute(other, 'img', [(i, i ^ 1) for i in range(devices)])  4.01 us
    pallas_call x1, Pallas kernels, shards(): pl.pallas_call(terms_kernel, name='terms', out_shape=(jax.ShapeDtypeStruc...  2.05 us
    ppermute x1, waiting for transfers between devices, shards(): other = lax.ppermute(other, 'img', [(i, i ^ 1) for i in range(devices)])  1.75 us
  transfers between devices with their start and end apart: 2, of which 2 were waited for; matrix products, arithmetic and copies ran while one was open for 0% of the time, Pallas kernels for 3%

commit v1 on v0

--- a/solution.py
+++ b/solution.py
@@ -13,7 +13,7 @@
 LANES = 128
 COLS = 256
 PAD = 8
-PARTS = 8
+NONE = -1e30
 BF = jnp.bfloat16
 F32 = jnp.float32
 
@@ -65,32 +65,30 @@
 
 
 def score_kernel(
-    far_pixels, far_proj, far_noise, far_defocus, far_counts, far_limits, scores, stats,
-    pixels, proj, noise, defocus, counts, limits, terms, terms_sq, turn, edge, arrived, small_arrived,
+    far_defocus, far_limits, far_pixels, far_proj, far_noise, far_counts, packed, stats,
+    defocus, limits, pixels, proj, noise, counts, terms, terms_sq, turn, edge, arrived,
 ):
     rows, images = proj.shape[0], pixels.shape[0]
-    small = [
-        pltpu.make_async_copy(far, near, small_arrived.at[k])
+    copies = [
+        pltpu.make_async_copy(far, near, arrived.at[k])
         for k, (far, near) in enumerate(
-            ((far_defocus, defocus), (far_limits, limits), (far_noise, noise), (far_counts, counts))
+            (
+                (far_defocus, defocus),
+                (far_limits, limits),
+                (far_pixels, pixels),
+                (far_proj, proj),
+                (far_noise, noise),
+                (far_counts, counts),
+            )
         )
     ]
-    for copy in small:
+    for copy in copies:
         copy.start()
-    copies = []
-    for n in range(PARTS):
-        at = pl.ds(n * (F // PARTS), F // PARTS)
-        copies.append(
-            [
-                pltpu.make_async_copy(far.at[:, at], near.at[:, at], arrived.at[k, n])
-                for k, (far, near) in enumerate(((far_pixels, pixels), (far_proj, proj)))
-            ]
-        )
-        for copy in copies[-1]:
-            copy.start()
-    for copy in small:
+    for copy in copies[:2]:
         copy.wait()
     set_turn(defocus[...], limits[...], turn, edge)
+    for copy in copies[2:]:
+        copy.wait()
 
     def use(some, at, inner, image, square):
         weight = noise[:, at]
@@ -99,11 +97,7 @@
 
     total = jnp.zeros((rows, images), F32)
     contract = (((1,), (1,)), ((), ()))
-    groups = F // COLS
-    for g in range(groups):
-        if g % (groups // PARTS) == 0:
-            for copy in copies[g // (groups // PARTS)]:
-                copy.wait()
+    for g in range(F // COLS):
         walk(g, pixels, turn, edge, use)
         at = slice(g * COLS, (g + 1) * COLS)
         some_proj = proj[:, at]
@@ -112,26 +106,46 @@
         total += lax.dot_general((wide * wide).astype(BF), terms_sq[:, at], contract, preferred_element_type=F32)
     orient = lax.axis_index("proj") * rows + lax.broadcasted_iota(jnp.int32, (rows, images), 0)
     significant = orient < counts[...]
-    found = jnp.where(significant, total, -1e30)
+    found = jnp.where(significant, total, NONE)
     peak = jnp.max(found, axis=0, keepdims=True)
     mass = jnp.sum(jnp.where(significant, jnp.exp(found - peak), 0.0), axis=0, keepdims=True)
-    scores[...] = found
     both = jnp.concatenate([peak, mass], axis=0)
     stats[...] = jnp.broadcast_to(both[None], stats.shape)
-
-
-def terms_kernel(far_pixels, defocus, limits, plan, back, chosen, pixels, turn, edge, arrived):
-    copy = pltpu.make_async_copy(far_pixels, pixels, arrived)
+    packed[:rows, :] = found
+    line = lax.broadcasted_iota(jnp.int32, (8, images), 0)
+    packed[rows:, :] = jnp.where(line == 0, defocus[...], jnp.where(line == 1, limits[...].astype(F32), 0.0))
+
+
+def terms_kernel(pixels, far_pixels, packed, other_packed, plan, back, chosen, other_pixels, turn, edge, arrived):
+    copy = pltpu.make_async_copy(far_pixels, other_pixels, arrived)
     copy.start()
-    set_turn(defocus[...], limits[...], turn, edge)
-    copy.wait()
-    for g in range(F // COLS):
-
-        def use(some, at, inner, image, square):
-            back[g, 0, some, inner] = image.astype(BF)
-            back[g, 1, some, inner] = square.astype(BF)
-
-        walk(g, pixels, turn, edge, use)
+    core = lax.rem(lax.axis_index("img"), 2)
+    images = pixels.shape[0]
+    rows = packed.shape[0] - 8
+    for part, (source, scalars) in enumerate(((pixels, packed), (other_pixels, other_packed))):
+        set_turn(scalars[rows : rows + 1, :], scalars[rows + 1 : rows + 2, :], turn, edge)
+        if part == 1:
+            copy.wait()
+        for r in range(0, images, 16):
+            some = slice(r, r + 16)
+            out = slice(part * images + r, part * images + r + 16)
+            s, before = turn[0, some], turn[1, some]
+            twice = turn[2, some]
+            one = twice * s - before
+            two = twice * one - s
+            s, before = jnp.where(core == 0, s, two), jnp.where(core == 0, before, one)
+            last = edge[some] - (core * COLS).astype(F32)
+            for y in range(back.shape[0]):
+                for h in range(COLS // LANES):
+                    first = 2 * y * COLS + h * LANES
+                    at = pl.ds(pl.multiple_of(first + core * COLS, LANES), LANES)
+                    inner = slice(h * LANES, (h + 1) * LANES)
+                    kept = jnp.where(last > float(first), s, 0.0)
+                    back[y, 0, out, inner] = (kept * source[some, at].astype(F32)).astype(BF)
+                    back[y, 1, out, inner] = (kept * s).astype(BF)
+                    s, before = twice * s - before, s
+                for h in range(COLS // LANES):
+                    s, before = twice * s - before, s
     per_line = LANES // BLOCK
     shape = chosen.shape[1:]
     blocks = plan.shape[1]
@@ -156,29 +170,36 @@
     return first, second, (rest - second.astype(F32)).astype(BF)
 
 
-def back_kernel(scores, stats, back, counts, own, other):
-    rows, images = scores.shape
+def evidence_of(stats):
     peaks, masses = stats[:, 0, :], stats[:, 1, :]
     peak = jnp.max(peaks, axis=0, keepdims=True)
     mass = jnp.sum(masses * jnp.exp(peaks - peak), axis=0, keepdims=True)
-    evidence = peak + jnp.log(mass)
-    orient = lax.axis_index("proj") * rows + lax.broadcasted_iota(jnp.int32, (rows, images), 0)
-    significant = orient < counts[...]
-    posterior = jnp.where(significant, jnp.exp(scores[...] - evidence), 0.0).astype(BF)
+    return peak + jnp.log(mass)
+
+
+def back_kernel(packed, other_packed, stats, back, out):
+    rows = packed.shape[0] - 8
+    peers = stats.shape[0] // 2
     core = lax.rem(lax.axis_index("img"), 2)
-    here = lax.broadcasted_iota(jnp.int32, (PAD, COLS), 1) // LANES == core
+    known = [evidence_of(stats[c * peers : (c + 1) * peers]) for c in range(2)]
+    mine, other = jnp.where(core == 0, known[0], known[1]), jnp.where(core == 0, known[1], known[0])
+    posterior = jnp.concatenate(
+        [
+            jnp.where(some[:rows, :] > 0.5 * NONE, jnp.exp(some[:rows, :] - evidence), 0.0).astype(BF)
+            for some, evidence in ((packed, mine), (other_packed, other))
+        ],
+        axis=1,
+    )
     line = lax.broadcasted_iota(jnp.int32, (PAD, COLS), 0)
-    wide = jnp.concatenate([evidence, evidence], axis=1)
     note = jnp.zeros((PAD, COLS), F32)
-    for k, part in enumerate(thirds(wide)):
+    for k, part in enumerate(thirds(jnp.concatenate(known, axis=1))):
         note = jnp.where(line == k, part.astype(F32), note)
-    note = jnp.where(here, note, 0.0).astype(BF)
-    for out, side in ((own, core), (other, 1 - core)):
-        for y in range(own.shape[0]):
-            for k in range(2):
-                part = jnp.dot(posterior, back[2 * y + side, k], preferred_element_type=F32)
-                out[y, k * rows : (k + 1) * rows, :] = part.astype(BF)
-            out[y, 2 * rows :, :] = note
+    note = note.astype(BF)
+    for y in range(out.shape[0]):
+        for k in range(2):
+            part = jnp.dot(posterior, back[y, k], preferred_element_type=F32)
+            out[y, k * rows : (k + 1) * rows, :] = part.astype(BF)
+        out[y, 2 * rows :, :] = note
 
 
 def last_kernel(parts, chosen, far_reconstruction, far_evidence, reconstruction, evidence, sent):
@@ -221,59 +242,54 @@
     rows, count = projections.shape[0], images.shape[0]
     devices, peers = lax.axis_size("img"), lax.axis_size("proj")
     chips = devices // 2
-    limit = pltpu.CompilerParams(vmem_limit_bytes=48 * 2**20)
-    counts = orient_count.reshape(1, count)
-    focus, limits = defocus.reshape(1, count), term_limit.reshape(1, count)
+    limit = pltpu.CompilerParams(vmem_limit_bytes=16 * 2**20)
+    focus, counts, limits = (a.reshape(1, count) for a in (defocus, orient_count, term_limit))
     tables = [pltpu.VMEM((3, count, LANES), F32), pltpu.VMEM((count, LANES), F32)]
-    scores, stats = pl.pallas_call(
+    partners = [(i, i ^ 1) for i in range(devices)]
+    other_images = lax.optimization_barrier(lax.ppermute(images, "img", partners))
+    operands = (focus, limits, images, projections, noise_weight.reshape(1, F), counts)
+    packed, stats = pl.pallas_call(
         score_kernel,
         name="score",
         out_shape=(
-            jax.ShapeDtypeStruct((rows, count), F32),
-            jax.ShapeDtypeStruct((peers, 2, count), F32),
+            jax.ShapeDtypeStruct((rows + 8, count), F32),
+            jax.ShapeDtypeStruct((2 * peers, 2, count), F32),
         ),
         in_specs=[pl.BlockSpec(memory_space=pltpu.HBM)] * 6,
         out_specs=tuple(vmem(2)),
         scratch_shapes=[
-            pltpu.VMEM((count, F), BF),
-            pltpu.VMEM((rows, F), BF),
-            pltpu.VMEM((1, F), F32),
-            pltpu.VMEM((1, count), F32),
-            pltpu.VMEM((1, count), jnp.int32),
-            pltpu.VMEM((1, count), jnp.int32),
+            *(pltpu.VMEM(a.shape, a.dtype) for a in operands),
             pltpu.VMEM((count, F), BF),
             pltpu.VMEM((count, F), BF),
             *tables,
-            pltpu.SemaphoreType.DMA((2, PARTS)),
-            pltpu.SemaphoreType.DMA((4,)),
+            pltpu.SemaphoreType.DMA((6,)),
         ],
         compiler_params=limit,
-    )(*map(kept_far, (images, projections, noise_weight.reshape(1, F), focus, counts, limits)))
+    )(*map(kept_far, operands))
+    chip = [[2 * y * peers + n for n in range(2 * peers)] for y in range(chips)]
+    stats = lax.all_to_all(stats, ("img", "proj"), 0, 0, tiled=True, axis_index_groups=chip)
+    other_packed = lax.ppermute(packed, "img", partners)
     back, chosen = pl.pallas_call(
         terms_kernel,
         name="terms",
         out_shape=(
-            jax.ShapeDtypeStruct((devices, 2, count, COLS), BF),
+            jax.ShapeDtypeStruct((chips, 2, 2 * count, COLS), BF),
             jax.ShapeDtypeStruct((LANES // BLOCK, devices, LANES), F32),
         ),
-        in_specs=[pl.BlockSpec(memory_space=pltpu.HBM), *vmem(3)],
+        in_specs=[*vmem(1), pl.BlockSpec(memory_space=pltpu.HBM), *vmem(3)],
         out_specs=tuple(vmem(2)),
         scratch_shapes=[pltpu.VMEM((count, F), BF), *tables, pltpu.SemaphoreType.DMA],
         compiler_params=limit,
         cost_estimate=pl.CostEstimate(flops=20 * count * F, bytes_accessed=6 * count * F, transcendentals=0),
-    )(kept_far(images), focus, limits, block_plan.reshape(1, -1))
-    stats = lax.all_to_all(stats, "proj", 0, 0, tiled=True)
-    shape = jax.ShapeDtypeStruct((chips, 2 * rows + PAD, COLS), BF)
-    own, other = pl.pallas_call(
+    )(images, kept_far(other_images), packed, other_packed, block_plan.reshape(1, -1))
+    both = pl.pallas_call(
         back_kernel,
         name="back",
-        out_shape=(shape, shape),
+        out_shape=jax.ShapeDtypeStruct((chips, 2 * rows + PAD, COLS), BF),
         in_specs=vmem(4),
-        out_specs=tuple(vmem(2)),
+        out_specs=vmem(1)[0],
         compiler_params=limit,
-    )(scores, stats, back, counts)
-    other = lax.ppermute(other, "img", [(i, i ^ 1) for i in range(devices)])
-    both = (own.astype(F32) + other.astype(F32)).astype(BF)
+    )(packed, other_packed, stats, back)
     same_core = [[2 * y + c for y in range(chips)] for c in range(2)]
     parts = lax.all_to_all(both, "img", 0, 0, tiled=True, axis_index_groups=same_core)
     reconstruction, evidence = pl.pallas_call(

time: 61.7 us -> 60.6 us (0.982)
  waiting for transfers between devices: 8.36 us -> 4.36 us
  starting transfers between devices: 17.7 us -> 19.4 us
  blocking collectives: 26.8 us -> 28 us
  local copies, waits for them, and re-layouts: 0.02 us -> 0.78 us
    ppermute x1 -> x2, starting transfers between devices: 4.01 us -> 11.2 us  [the longest x1 8.92 us: shards(): lax.ppermute(images, 'img', partners)]
    all_to_all x1, starting transfers between devices: 13.7 us -> 8.18 us  [shards(): lax.all_to_all(stats, ('img', 'proj'), 0, 0, tiled=True, axis_index_group...]
    all_to_all x1, waiting for transfers between devices: 6.61 us -> 3.52 us  [shards(): lax.all_to_all(stats, ('img', 'proj'), 0, 0, tiled=True, axis_index_group...]
    all_to_all x1, blocking collectives: 26.8 us -> 28 us  [shards(): lax.all_to_all(both, 'img', 0, 0, tiled=True, axis_index_groups=same_core)]
    ppermute x1 -> x2, waiting for transfers between devices: 1.75 us -> 0.84 us  [the longest x1 0.83 us: shards(): other_packed = lax.ppermute(packed, 'img', partners)]
    unnamed x8 -> x6, local copies, waits for them, and re-layouts: 0.02 us -> 0.78 us
  transfers between devices with their start and end apart: 2 -> 3, of which waited for: 2 -> 2; matrix products, arithmetic and copies ran while one was open for 0% -> 0% of each run, Pallas kernels for 3% -> 10%
where the time goes in v1:
time: 60.6 us; the launch traced here: 60.3 us
  blocking collectives  28 us (46%)
  starting transfers between devices  19.4 us (32%)
  Pallas kernels  7.12 us (12%)
  waiting for transfers between devices  4.36 us (7%)
  local copies, waits for them, and re-layouts  0.78 us (1%)
  between operations  0.7 us (1%)
    all_to_all x1, blocking collectives, shards(): lax.all_to_all(both, 'img', 0, 0, tiled=True, axis_index_groups=same_core)  28 us
    ppermute x1, starting transfers between devices, shards(): lax.ppermute(images, 'img', partners)  8.92 us
    all_to_all x1, starting transfers between devices, shards(): lax.all_to_all(stats, ('img', 'proj'), 0, 0, tiled=True, axis_index_group...  8.18 us
    pallas_call x1, Pallas kernels, shards(): pl.pallas_call(score_kernel, name='score', out_shape=(jax.ShapeDtypeStruc...  3.67 us
    all_to_all x1, waiting for transfers between devices, shards(): lax.all_to_all(stats, ('img', 'proj'), 0, 0, tiled=True, axis_index_group...  3.52 us
    ppermute x1, starting transfers between devices, shards(): other_packed = lax.ppermute(packed, 'img', partners)  2.26 us
    pallas_call x1, Pallas kernels, shards(): pl.pallas_call(terms_kernel, name='terms', out_shape=(jax.ShapeDtypeStruc...  2.14 us
  transfers between devices with their start and end apart: 3, of which 2 were waited for; matrix products, arithmetic and copies ran while one was open for 0% of the time, Pallas kernels for 10%

profile of v1, /device:TPU:1, one launch (start us, length us, event | category | flops | bytes accessed | tf_op | source)
XLA Modules:
  0.0 60.3 jit_solution(8933889701046958115)
XLA Ops:
  0.6 0.0 copy-start
  0.6 8.9 %collective-permute-start.1 = (bf16[128,4096]{1,0:T(8,128)(2,1)}, bf16[128,4096]{1,0:T(8,128)(2,1)S(1)}, u32[]{:S(2)}, u32[]{:S(2)}) collective-permute-start(bf16[128,4096]{1,0:T(8,128)(2,1)} %pixels.1), channel_id=1, source_target_pairs={{0,32},{32,0},{64,96},{96,64},{128,160},{160,128},{192,224},{224,1... | collective-permute-start | bytes 3145736 | tf_op jit(solution)/shard_map/ppermute | solution.py:249
  9.6 3.7 %score.1 = (f32[88,128]{1,0:T(8,128)S(1)}, f32[64,2,128]{2,1,0:T(2,128)}) custom-call(f32[1,128]{1,0:T(1,128)} %bitcast.8, s32[1,128]{1,0:T(1,128)} %bitcast.9, bf16[128,4096]{1,0:T(8,128)(2,1)} %pixels.1, bf16[80,4096]{1,0:T(8,128)(2,1)} %far_proj.1, f32[1,4096]{1,0:T(1,128)} %bitcast.7, s32[1,128]{1,0:T(1,128)} %bitcast.10), custom_call_target="tpu_custom_call" | custom-call | tf_op jit(solution)/shard_map/score/pallas_call | solution.py:251
  13.2 8.2 %all-to-all-start = ((f32[64,2,128]{2,1,0:T(2,128)}), f32[64,2,128]{2,1,0:T(2,128)S(1)}, u32[]{:S(2)}, u32[]{:S(2)}) async-start(f32[64,2,128]{2,1,0:T(2,128)} %get-tuple-element.9), calls=%async_computation | async-start | bytes 131072 | tf_op jit(solution)/shard_map/all_to_all | solution.py:270
  21.4 2.3 %collective-permute-start = (f32[88,128]{1,0:T(8,128)S(1)}, f32[88,128]{1,0:T(8,128)S(1)}, u32[]{:S(2)}, u32[]{:S(2)}) collective-permute-start(f32[88,128]{1,0:T(8,128)S(1)} %get-tuple-element.8.packed), channel_id=1, source_target_pairs={{0,32},{32,0},{64,96},{96,64},{128,160},{160,128},{192,224},{224,1... | collective-permute-start | bytes 135176 | tf_op jit(solution)/shard_map/ppermute | solution.py:271
  23.7 0.0 collective-permute-done.1.far_pixels
  23.7 0.0 copy-start.2
  23.7 0.8 %collective-permute-done.other_packed = f32[88,128]{1,0:T(8,128)S(1)} collective-permute-done((f32[88,128]{1,0:T(8,128)S(1)}, f32[88,128]{1,0:T(8,128)S(1)}, u32[]{:S(2)}, u32[]{:S(2)}) %collective-permute-start) | collective-permute-done | bytes 45088 | tf_op jit(solution)/shard_map/ppermute | solution.py:271
  24.6 0.1 copy-done.2
  24.7 0.0 copy-done
  24.7 0.0 copy-start.1
  24.7 0.7 %copy-done.1 = s32[64]{0:T(128)S(1)} copy-done((s32[64]{0:T(128)S(1)}, s32[64]{0:T(128)}, u32[]{:S(2)}) %copy-start.1) | copy-done | bytes 280
  25.3 2.1 %terms.1 = (bf16[8,2,256,256]{3,2,1,0:T(8,128)(2,1)S(1)}, f32[4,16,128]{2,1,0:T(8,128)S(1)}) custom-call(bf16[128,4096]{1,0:T(8,128)(2,1)S(1)} %copy-done, bf16[128,4096]{1,0:T(8,128)(2,1)} %copy-done.2, f32[88,128]{1,0:T(8,128)S(1)} %get-tuple-element.8.packed, f32[88,128]{1,0:T(8,128)S(1)} %collective-permute-done.other_packed, s32[1,64]{1,0:T(1,128)S(1)} %bitcast.6), custom_call_target="tpu_custom_call" | custom-call | flops 10485760 | bytes 3145728 | tf_op jit(solution)/shard_map/terms/pallas_call | solution.py:272
  27.5 3.5 %all-to-all-done.stats = f32[64,2,128]{2,1,0:T(2,128)S(1)} async-done(((f32[64,2,128]{2,1,0:T(2,128)}), f32[64,2,128]{2,1,0:T(2,128)S(1)}, u32[]{:S(2)}, u32[]{:S(2)}) %all-to-all-start) | async-done | bytes 65568 | tf_op jit(solution)/shard_map/all_to_all | solution.py:270
  31.0 0.6 back.1
  31.6 28.0 %all_to_all.10.parts = bf16[8,168,256]{2,1,0:T(8,128)(2,1)S(1)} all-to-all(bf16[8,168,256]{2,1,0:T(8,128)(2,1)S(1)} %back.1), channel_id=1, replica_groups={{0,64,128,192,256,320,384,448},{32,96,160,224,288,352,416,480},{1,65,12..., dimensions={0} | all-to-all | bytes 1376256 | tf_op jit(solution)/shard_map/all_to_all | solution.py:294
  59.6 0.7 %last.1 = (bf16[80,256]{1,0:T(8,128)(2,1)}, f32[1,128]{1,0:T(1,128)}) custom-call(bf16[8,168,256]{2,1,0:T(8,128)(2,1)S(1)} %all_to_all.10.parts, f32[4,16,128]{2,1,0:T(8,128)S(1)} %get-tuple-element.11.chosen), custom_call_target="tpu_custom_call" | custom-call | tf_op jit(solution)/shard_map/last/pallas_call | solution.py:295
Async XLA Ops:
  0.6 24.0 %copy-start = (bf16[128,4096]{1,0:T(8,128)(2,1)S(1)}, bf16[128,4096]{1,0:T(8,128)(2,1)}, u32[]{:S(2)}) copy-start(bf16[128,4096]{1,0:T(8,128)(2,1)} %pixels.1) | copy-start | bytes 3145732
  0.6 23.1 %collective-permute-start.1 = (bf16[128,4096]{1,0:T(8,128)(2,1)}, bf16[128,4096]{1,0:T(8,128)(2,1)S(1)}, u32[]{:S(2)}, u32[]{:S(2)}) collective-permute-start(bf16[128,4096]{1,0:T(8,128)(2,1)} %pixels.1), channel_id=1, source_target_pairs={{0,32},{32,0},{64,96},{96,64},{128,160},{160,128},{192,224},{224,1... | collective-permute-start | bytes 3145736 | tf_op jit(solution)/shard_map/ppermute | solution.py:249
  13.2 17.8 %all-to-all-start = ((f32[64,2,128]{2,1,0:T(2,128)}), f32[64,2,128]{2,1,0:T(2,128)S(1)}, u32[]{:S(2)}, u32[]{:S(2)}) async-start(f32[64,2,128]{2,1,0:T(2,128)} %get-tuple-element.9), calls=%async_computation | async-start | bytes 131072 | tf_op jit(solution)/shard_map/all_to_all | solution.py:270
  21.4 3.1 %collective-permute-start = (f32[88,128]{1,0:T(8,128)S(1)}, f32[88,128]{1,0:T(8,128)S(1)}, u32[]{:S(2)}, u32[]{:S(2)}) collective-permute-start(f32[88,128]{1,0:T(8,128)S(1)} %get-tuple-element.8.packed), channel_id=1, source_target_pairs={{0,32},{32,0},{64,96},{96,64},{128,160},{160,128},{192,224},{224,1... | collective-permute-start | bytes 135176 | tf_op jit(solution)/shard_map/ppermute | solution.py:271
  23.7 1.0 %copy-start.2 = (bf16[128,4096]{1,0:T(8,128)(2,1)}, bf16[128,4096]{1,0:T(8,128)(2,1)S(1)}, u32[]{:S(2)}) copy-start(bf16[128,4096]{1,0:T(8,128)(2,1)S(1)} %collective-permute-done.1.far_pixels) | copy-start | bytes 3145732
  24.7 0.7 %copy-start.1 = (s32[64]{0:T(128)S(1)}, s32[64]{0:T(128)}, u32[]{:S(2)}) copy-start(s32[64]{0:T(128)} %param.13) | copy-start | bytes 772

commit v2 on v1

--- a/solution.py
+++ b/solution.py
@@ -64,8 +64,15 @@
         turn[0, some], turn[1, some] = s, before
 
 
+def thirds(x):
+    first = x.astype(BF)
+    rest = x - first.astype(F32)
+    second = rest.astype(BF)
+    return first, second, (rest - second.astype(F32)).astype(BF)
+
+
 def score_kernel(
-    far_defocus, far_limits, far_pixels, far_proj, far_noise, far_counts, packed, stats,
+    far_defocus, far_limits, far_pixels, far_proj, far_noise, far_counts, kept, sent, stats,
     defocus, limits, pixels, proj, noise, counts, terms, terms_sq, turn, edge, arrived,
 ):
     rows, images = proj.shape[0], pixels.shape[0]
@@ -111,41 +118,66 @@
     mass = jnp.sum(jnp.where(significant, jnp.exp(found - peak), 0.0), axis=0, keepdims=True)
     both = jnp.concatenate([peak, mass], axis=0)
     stats[...] = jnp.broadcast_to(both[None], stats.shape)
-    packed[:rows, :] = found
-    line = lax.broadcasted_iota(jnp.int32, (8, images), 0)
-    packed[rows:, :] = jnp.where(line == 0, defocus[...], jnp.where(line == 1, limits[...].astype(F32), 0.0))
-
-
-def terms_kernel(pixels, far_pixels, packed, other_packed, plan, back, chosen, other_pixels, turn, edge, arrived):
-    copy = pltpu.make_async_copy(far_pixels, other_pixels, arrived)
+    line = lax.broadcasted_iota(jnp.int32, (rows, images), 0)
+    scalars = jnp.zeros((rows, images), F32)
+    for k, part in enumerate((*thirds(defocus[...]), *thirds(limits[...].astype(F32)))):
+        scalars = jnp.where(line == k, part.astype(F32), scalars)
+    first, second, third = thirds(found)
+    core = lax.rem(lax.axis_index("img"), 2)
+    groups = F // COLS // 2
+    tail = groups * images
+    for out, side in ((kept, core), (sent, 1 - core)):
+        for y in range(groups):
+            at = pl.ds(pl.multiple_of((2 * y + side) * COLS, COLS), COLS)
+            out[y * images : (y + 1) * images, :] = pixels[:, at]
+        out[tail : tail + rows, :LANES] = first
+        out[tail : tail + rows, LANES:] = second
+        out[tail + rows :, :LANES] = third
+        out[tail + rows :, LANES:] = scalars.astype(BF)
+
+
+def scores_of(half, rows):
+    tail = half.shape[0] - 2 * rows
+    first, second = half[tail : tail + rows, :LANES], half[tail : tail + rows, LANES:]
+    return (first.astype(F32) + second.astype(F32)) + half[tail + rows :, :LANES].astype(F32)
+
+
+def half_terms(half, rows, back, turn, edge):
+    core = lax.rem(lax.axis_index("img"), 2)
+    images = back.shape[2]
+    start = half.shape[0] - rows
+    scalars = half[start : start + 16, LANES:].astype(F32)
+    focus, limits = ((scalars[k : k + 1] + scalars[k + 1 : k + 2]) + scalars[k + 2 : k + 3] for k in (0, 3))
+    set_turn(focus, limits, turn, edge)
+    for r in range(0, images, 16):
+        some = slice(r, r + 16)
+        s, before = turn[0, some], turn[1, some]
+        twice = turn[2, some]
+        one = twice * s - before
+        two = twice * one - s
+        s, before = jnp.where(core == 0, s, two), jnp.where(core == 0, before, one)
+        last = edge[some] - (core * COLS).astype(F32)
+        for y in range(back.shape[0]):
+            for h in range(COLS // LANES):
+                inner = slice(h * LANES, (h + 1) * LANES)
+                kept = jnp.where(last > float(2 * y * COLS + h * LANES), s, 0.0)
+                image = half[y * images + r : y * images + r + 16, inner].astype(F32)
+                back[y, 0, some, inner] = (kept * image).astype(BF)
+                back[y, 1, some, inner] = (kept * s).astype(BF)
+                s, before = twice * s - before, s
+            for h in range(COLS // LANES):
+                s, before = twice * s - before, s
+
+
+def other_terms_kernel(rows, half, back, turn, edge):
+    half_terms(half, rows, back, turn, edge)
+
+
+def own_terms_kernel(rows, half, far_plan, back, chosen, plan, turn, edge, arrived):
+    copy = pltpu.make_async_copy(far_plan, plan, arrived)
     copy.start()
-    core = lax.rem(lax.axis_index("img"), 2)
-    images = pixels.shape[0]
-    rows = packed.shape[0] - 8
-    for part, (source, scalars) in enumerate(((pixels, packed), (other_pixels, other_packed))):
-        set_turn(scalars[rows : rows + 1, :], scalars[rows + 1 : rows + 2, :], turn, edge)
-        if part == 1:
-            copy.wait()
-        for r in range(0, images, 16):
-            some = slice(r, r + 16)
-            out = slice(part * images + r, part * images + r + 16)
-            s, before = turn[0, some], turn[1, some]
-            twice = turn[2, some]
-            one = twice * s - before
-            two = twice * one - s
-            s, before = jnp.where(core == 0, s, two), jnp.where(core == 0, before, one)
-            last = edge[some] - (core * COLS).astype(F32)
-            for y in range(back.shape[0]):
-                for h in range(COLS // LANES):
-                    first = 2 * y * COLS + h * LANES
-                    at = pl.ds(pl.multiple_of(first + core * COLS, LANES), LANES)
-                    inner = slice(h * LANES, (h + 1) * LANES)
-                    kept = jnp.where(last > float(first), s, 0.0)
-                    back[y, 0, out, inner] = (kept * source[some, at].astype(F32)).astype(BF)
-                    back[y, 1, out, inner] = (kept * s).astype(BF)
-                    s, before = twice * s - before, s
-                for h in range(COLS // LANES):
-                    s, before = twice * s - before, s
+    half_terms(half, rows, back, turn, edge)
+    copy.wait()
     per_line = LANES // BLOCK
     shape = chosen.shape[1:]
     blocks = plan.shape[1]
@@ -163,13 +195,6 @@
         chosen[k] = jnp.where(moved == slot, 1.0, 0.0)
 
 
-def thirds(x):
-    first = x.astype(BF)
-    rest = x - first.astype(F32)
-    second = rest.astype(BF)
-    return first, second, (rest - second.astype(F32)).astype(BF)
-
-
 def evidence_of(stats):
     peaks, masses = stats[:, 0, :], stats[:, 1, :]
     peak = jnp.max(peaks, axis=0, keepdims=True)
@@ -177,19 +202,18 @@
     return peak + jnp.log(mass)
 
 
-def back_kernel(packed, other_packed, stats, back, out):
-    rows = packed.shape[0] - 8
+def back_kernel(half, other_half, stats, back, other_back, out):
+    rows = (out.shape[1] - PAD) // 2
     peers = stats.shape[0] // 2
     core = lax.rem(lax.axis_index("img"), 2)
     known = [evidence_of(stats[c * peers : (c + 1) * peers]) for c in range(2)]
     mine, other = jnp.where(core == 0, known[0], known[1]), jnp.where(core == 0, known[1], known[0])
-    posterior = jnp.concatenate(
-        [
-            jnp.where(some[:rows, :] > 0.5 * NONE, jnp.exp(some[:rows, :] - evidence), 0.0).astype(BF)
-            for some, evidence in ((packed, mine), (other_packed, other))
-        ],
-        axis=1,
-    )
+
+    def posterior_of(scores, evidence):
+        return jnp.where(scores > 0.5 * NONE, jnp.exp(scores - evidence), 0.0).astype(BF)
+
+    posterior = posterior_of(scores_of(half, rows), mine)
+    other_posterior = posterior_of(scores_of(other_half, rows), other)
     line = lax.broadcasted_iota(jnp.int32, (PAD, COLS), 0)
     note = jnp.zeros((PAD, COLS), F32)
     for k, part in enumerate(thirds(jnp.concatenate(known, axis=1))):
@@ -198,6 +222,7 @@
     for y in range(out.shape[0]):
         for k in range(2):
             part = jnp.dot(posterior, back[y, k], preferred_element_type=F32)
+            part += jnp.dot(other_posterior, other_back[y, k], preferred_element_type=F32)
             out[y, k * rows : (k + 1) * rows, :] = part.astype(BF)
         out[y, 2 * rows :, :] = note
 
@@ -246,17 +271,18 @@
     focus, counts, limits = (a.reshape(1, count) for a in (defocus, orient_count, term_limit))
     tables = [pltpu.VMEM((3, count, LANES), F32), pltpu.VMEM((count, LANES), F32)]
     partners = [(i, i ^ 1) for i in range(devices)]
-    other_images = lax.optimization_barrier(lax.ppermute(images, "img", partners))
     operands = (focus, limits, images, projections, noise_weight.reshape(1, F), counts)
-    packed, stats = pl.pallas_call(
+    shape = jax.ShapeDtypeStruct((chips * count + 2 * rows, COLS), BF)
+    half, sent, stats = pl.pallas_call(
         score_kernel,
         name="score",
         out_shape=(
-            jax.ShapeDtypeStruct((rows + 8, count), F32),
+            shape,
+            shape,
             jax.ShapeDtypeStruct((2 * peers, 2, count), F32),
         ),
         in_specs=[pl.BlockSpec(memory_space=pltpu.HBM)] * 6,
-        out_specs=tuple(vmem(2)),
+        out_specs=tuple(vmem(3)),
         scratch_shapes=[
             *(pltpu.VMEM(a.shape, a.dtype) for a in operands),
             pltpu.VMEM((count, F), BF),
@@ -268,28 +294,37 @@
     )(*map(kept_far, operands))
     chip = [[2 * y * peers + n for n in range(2 * peers)] for y in range(chips)]
     stats = lax.all_to_all(stats, ("img", "proj"), 0, 0, tiled=True, axis_index_groups=chip)
-    other_packed = lax.ppermute(packed, "img", partners)
+    shape = jax.ShapeDtypeStruct((chips, 2, count, COLS), BF)
+    cost = pl.CostEstimate(flops=10 * count * F, bytes_accessed=3 * count * F, transcendentals=0)
     back, chosen = pl.pallas_call(
-        terms_kernel,
-        name="terms",
-        out_shape=(
-            jax.ShapeDtypeStruct((chips, 2, 2 * count, COLS), BF),
-            jax.ShapeDtypeStruct((LANES // BLOCK, devices, LANES), F32),
-        ),
-        in_specs=[*vmem(1), pl.BlockSpec(memory_space=pltpu.HBM), *vmem(3)],
+        functools.partial(own_terms_kernel, rows),
+        name="own_terms",
+        out_shape=(shape, jax.ShapeDtypeStruct((LANES // BLOCK, devices, LANES), F32)),
+        in_specs=[*vmem(1), pl.BlockSpec(memory_space=pltpu.HBM)],
         out_specs=tuple(vmem(2)),
-        scratch_shapes=[pltpu.VMEM((count, F), BF), *tables, pltpu.SemaphoreType.DMA],
-        compiler_params=limit,
-        cost_estimate=pl.CostEstimate(flops=20 * count * F, bytes_accessed=6 * count * F, transcendentals=0),
-    )(images, kept_far(other_images), packed, other_packed, block_plan.reshape(1, -1))
+        scratch_shapes=[pltpu.VMEM((1, block_plan.shape[0]), jnp.int32), *tables, pltpu.SemaphoreType.DMA],
+        compiler_params=limit,
+        cost_estimate=cost,
+    )(half, kept_far(block_plan.reshape(1, -1)))
+    other_half = lax.ppermute(sent, "img", partners)
+    other_back = pl.pallas_call(
+        functools.partial(other_terms_kernel, rows),
+        name="other_terms",
+        out_shape=shape,
+        in_specs=vmem(1),
+        out_specs=vmem(1)[0],
+        scratch_shapes=tables,
+        compiler_params=limit,
+        cost_estimate=pl.CostEstimate(flops=1, bytes_accessed=1, transcendentals=0),
+    )(other_half)
     both = pl.pallas_call(
         back_kernel,
         name="back",
         out_shape=jax.ShapeDtypeStruct((chips, 2 * rows + PAD, COLS), BF),
-        in_specs=vmem(4),
+        in_specs=vmem(5),
         out_specs=vmem(1)[0],
         compiler_params=limit,
-    )(packed, other_packed, stats, back)
+    )(half, other_half, stats, back, other_back)
     same_core = [[2 * y + c for y in range(chips)] for c in range(2)]
     parts = lax.all_to_all(both, "img", 0, 0, tiled=True, axis_index_groups=same_core)
     reconstruction, evidence = pl.pallas_call(

time: 60.6 us -> 60.5 us (level)
  waiting for transfers between devices: 4.36 us -> 8.1 us
  starting transfers between devices: 19.4 us -> 17 us
  local copies, waits for them, and re-layouts: 0.78 us -> 0 us
  Pallas kernels: 7.12 us -> 6.42 us
    all_to_all x1, waiting for transfers between devices: 3.52 us -> 8.1 us  [shards(): lax.all_to_all(stats, ('img', 'proj'), 0, 0, tiled=True, axis_index_group...]
    ppermute x2 -> x1, starting transfers between devices: 11.2 us -> 8.79 us  [shards(): other_half = lax.ppermute(sent, 'img', partners)]
    ppermute x2 -> x1, waiting for transfers between devices: 0.84 us -> 0.01 us  [shards(): other_half = lax.ppermute(sent, 'img', partners)]
    unnamed x6 -> x0, local copies, waits for them, and re-layouts: 0.78 us -> none
    pallas_call x2 -> x3, Pallas kernels: 5.81 us -> 5.11 us  [the longest x1 3.66 us: shards(): pl.pallas_call(score_kernel, name='score', out_shape=(shape, shape, jax.S...]
  transfers between devices with their start and end apart: 3 -> 2, of which waited for: 2 -> 1; matrix products, arithmetic and copies ran while one was open for 0% -> 0% of each run, Pallas kernels for 10% -> 2%
where the time goes in v2:
time: 60.5 us; the launch traced here: 60.2 us
  blocking collectives  28 us (46%)
  starting transfers between devices  17 us (28%)
  waiting for transfers between devices  8.1 us (13%)
  Pallas kernels  6.42 us (11%)
  between operations  0.69 us (1%)
    all_to_all x1, blocking collectives, shards(): lax.all_to_all(both, 'img', 0, 0, tiled=True, axis_index_groups=same_core)  28 us
    ppermute x1, starting transfers between devices, shards(): other_half = lax.ppermute(sent, 'img', partners)  8.79 us
    all_to_all x1, starting transfers between devices, shards(): lax.all_to_all(stats, ('img', 'proj'), 0, 0, tiled=True, axis_index_group...  8.18 us
    all_to_all x1, waiting for transfers between devices, shards(): lax.all_to_all(stats, ('img', 'proj'), 0, 0, tiled=True, axis_index_group...  8.1 us
    pallas_call x1, Pallas kernels, shards(): pl.pallas_call(score_kernel, name='score', out_shape=(shape, shape, jax.S...  3.66 us
  transfers between devices with their start and end apart: 2, of which 1 were waited for; matrix products, arithmetic and copies ran while one was open for 0% of the time, Pallas kernels for 2%

profile of v2, /device:TPU:1, one launch (start us, length us, event | category | flops | bytes accessed | tf_op | source)
XLA Modules:
  0.0 60.2 jit_solution(9663841325245550618)
XLA Ops:
  0.6 3.7 %score.1 = (bf16[1184,256]{1,0:T(8,128)(2,1)S(1)}, bf16[1184,256]{1,0:T(8,128)(2,1)S(1)}, f32[64,2,128]{2,1,0:T(2,128)}) custom-call(f32[1,128]{1,0:T(1,128)} %bitcast.7, s32[1,128]{1,0:T(1,128)} %bitcast.8, bf16[128,4096]{1,0:T(8,128)(2,1)} %far_pixels.1, bf16[80,4096]{1,0:T(8,128)(2,1)} %far_proj.1, f32[1,4096]{1,0:T(1,128)} %bitcast.6, s32[1,128]{1,0:T(1,128)} %bitcast.9), custom_call_target="tpu_custom_call" | custom-call | tf_op jit(solution)/shard_map/score/pallas_call | solution.py:276
  4.3 8.8 %collective-permute-start = (bf16[1184,256]{1,0:T(8,128)(2,1)S(1)}, bf16[1184,256]{1,0:T(8,128)(2,1)S(1)}, u32[]{:S(2)}, u32[]{:S(2)}) collective-permute-start(bf16[1184,256]{1,0:T(8,128)(2,1)S(1)} %get-tuple-element.10), channel_id=1, source_target_pairs={{0,32},{32,0},{64,96},{96,64},{128,160},{160,128},{192,224},{224,1... | collective-permute-start | bytes 1818632 | tf_op jit(solution)/shard_map/ppermute | solution.py:309
  13.1 8.2 %all-to-all-start = ((f32[64,2,128]{2,1,0:T(2,128)}), f32[64,2,128]{2,1,0:T(2,128)S(1)}, u32[]{:S(2)}, u32[]{:S(2)}) async-start(f32[64,2,128]{2,1,0:T(2,128)} %get-tuple-element.11), calls=%async_computation | async-start | bytes 131072 | tf_op jit(solution)/shard_map/all_to_all | solution.py:296
  21.3 0.8 %own_terms.1 = (bf16[8,2,128,256]{3,2,1,0:T(8,128)(2,1)S(1)}, f32[4,16,128]{2,1,0:T(8,128)S(1)}) custom-call(bf16[1184,256]{1,0:T(8,128)(2,1)S(1)} %get-tuple-element.9.half, s32[1,64]{1,0:T(1,128)} %bitcast.10), custom_call_target="tpu_custom_call" | custom-call | flops 5242880 | bytes 1572864 | tf_op jit(solution)/shard_map/own_terms/pallas_call | solution.py:299
  22.1 0.0 collective-permute-done.half.other_half
  22.1 0.6 %other_terms.1.other_back = bf16[8,2,128,256]{3,2,1,0:T(8,128)(2,1)S(1)} custom-call(bf16[1184,256]{1,0:T(8,128)(2,1)S(1)} %collective-permute-done.half.other_half), custom_call_target="tpu_custom_call" | custom-call | flops 1 | bytes 1 | tf_op jit(solution)/shard_map/other_terms/pallas_call | solution.py:310
  22.8 8.1 %all-to-all-done.stats = f32[64,2,128]{2,1,0:T(2,128)S(1)} async-done(((f32[64,2,128]{2,1,0:T(2,128)}), f32[64,2,128]{2,1,0:T(2,128)S(1)}, u32[]{:S(2)}, u32[]{:S(2)}) %all-to-all-start) | async-done | bytes 65568 | tf_op jit(solution)/shard_map/all_to_all | solution.py:296
  30.9 0.6 back.1
  31.4 28.0 %all_to_all.10.parts = bf16[8,168,256]{2,1,0:T(8,128)(2,1)S(1)} all-to-all(bf16[8,168,256]{2,1,0:T(8,128)(2,1)S(1)} %back.1), channel_id=1, replica_groups={{0,64,128,192,256,320,384,448},{32,96,160,224,288,352,416,480},{1,65,12..., dimensions={0} | all-to-all | bytes 1376256 | tf_op jit(solution)/shard_map/all_to_all | solution.py:329
  59.5 0.7 %last.1 = (bf16[80,256]{1,0:T(8,128)(2,1)}, f32[1,128]{1,0:T(1,128)}) custom-call(bf16[8,168,256]{2,1,0:T(8,128)(2,1)S(1)} %all_to_all.10.parts, f32[4,16,128]{2,1,0:T(8,128)S(1)} %get-tuple-element.13.chosen), custom_call_target="tpu_custom_call" | custom-call | tf_op jit(solution)/shard_map/last/pallas_call | solution.py:330
Async XLA Ops:
  4.3 17.8 %collective-permute-start = (bf16[1184,256]{1,0:T(8,128)(2,1)S(1)}, bf16[1184,256]{1,0:T(8,128)(2,1)S(1)}, u32[]{:S(2)}, u32[]{:S(2)}) collective-permute-start(bf16[1184,256]{1,0:T(8,128)(2,1)S(1)} %get-tuple-element.10), channel_id=1, source_target_pairs={{0,32},{32,0},{64,96},{96,64},{128,160},{160,128},{192,224},{224,1... | collective-permute-start | bytes 1818632 | tf_op jit(solution)/shard_map/ppermute | solution.py:309
  13.1 17.8 %all-to-all-start = ((f32[64,2,128]{2,1,0:T(2,128)}), f32[64,2,128]{2,1,0:T(2,128)S(1)}, u32[]{:S(2)}, u32[]{:S(2)}) async-start(f32[64,2,128]{2,1,0:T(2,128)} %get-tuple-element.11), calls=%async_computation | async-start | bytes 131072 | tf_op jit(solution)/shard_map/all_to_all | solution.py:296

commit v3 on v2

--- a/solution.py
+++ b/solution.py
@@ -102,15 +102,16 @@
         terms[some, at] = (weight * image).astype(BF)
         terms_sq[some, at] = ((-0.5 * weight) * square).astype(BF)
 
-    total = jnp.zeros((rows, images), F32)
+    sums = [jnp.zeros((rows, images), F32) for _ in range(4)]
     contract = (((1,), (1,)), ((), ()))
     for g in range(F // COLS):
         walk(g, pixels, turn, edge, use)
         at = slice(g * COLS, (g + 1) * COLS)
         some_proj = proj[:, at]
         wide = some_proj.astype(F32)
-        total += lax.dot_general(some_proj, terms[:, at], contract, preferred_element_type=F32)
-        total += lax.dot_general((wide * wide).astype(BF), terms_sq[:, at], contract, preferred_element_type=F32)
+        sums[g % 2] += lax.dot_general(some_proj, terms[:, at], contract, preferred_element_type=F32)
+        sums[2 + g % 2] += lax.dot_general((wide * wide).astype(BF), terms_sq[:, at], contract, preferred_element_type=F32)
+    total = (sums[0] + sums[1]) + (sums[2] + sums[3])
     orient = lax.axis_index("proj") * rows + lax.broadcasted_iota(jnp.int32, (rows, images), 0)
     significant = orient < counts[...]
     found = jnp.where(significant, total, NONE)
@@ -295,7 +296,7 @@
     chip = [[2 * y * peers + n for n in range(2 * peers)] for y in range(chips)]
     stats = lax.all_to_all(stats, ("img", "proj"), 0, 0, tiled=True, axis_index_groups=chip)
     shape = jax.ShapeDtypeStruct((chips, 2, count, COLS), BF)
-    cost = pl.CostEstimate(flops=10 * count * F, bytes_accessed=3 * count * F, transcendentals=0)
+    cost = pl.CostEstimate(flops=10**10, bytes_accessed=3 * count * F, transcendentals=0)
     back, chosen = pl.pallas_call(
         functools.partial(own_terms_kernel, rows),
         name="own_terms",

time: 60.5 us -> 58.4 us (0.965)
  waiting for transfers between devices: 8.1 us -> 5.84 us
    all_to_all x1, starting transfers between devices: 8.18 us -> 14.9 us  [shards(): lax.all_to_all(stats, ('img', 'proj'), 0, 0, tiled=True, axis_index_group...]
    ppermute x1, starting transfers between devices: 8.79 us -> 2.26 us  [shards(): other_half = lax.ppermute(sent, 'img', partners)]
    all_to_all x1, waiting for transfers between devices: 8.1 us -> 5.04 us  [shards(): lax.all_to_all(stats, ('img', 'proj'), 0, 0, tiled=True, axis_index_group...]
    ppermute x1, waiting for transfers between devices: 0.01 us -> 0.8 us  [shards(): other_half = lax.ppermute(sent, 'img', partners)]
  transfers between devices with their start and end apart: 2 -> 2, of which waited for: 1 -> 2; matrix products, arithmetic and copies ran while one was open for 0% -> 0% of each run, Pallas kernels for 2% -> 2%
where the time goes in v3:
time: 58.4 us; the launch traced here: 58.1 us
  blocking collectives  28 us (48%)
  starting transfers between devices  17.2 us (29%)
  Pallas kernels  6.38 us (11%)
  waiting for transfers between devices  5.84 us (10%)
  between operations  0.68 us (1%)
    all_to_all x1, blocking collectives, shards(): lax.all_to_all(both, 'img', 0, 0, tiled=True, axis_index_groups=same_core)  28 us
    all_to_all x1, starting transfers between devices, shards(): lax.all_to_all(stats, ('img', 'proj'), 0, 0, tiled=True, axis_index_group...  14.9 us
    all_to_all x1, waiting for transfers between devices, shards(): lax.all_to_all(stats, ('img', 'proj'), 0, 0, tiled=True, axis_index_group...  5.04 us
    pallas_call x1, Pallas kernels, shards(): pl.pallas_call(score_kernel, name='score', out_shape=(shape, shape, jax.S...  3.63 us
    ppermute x1, starting transfers between devices, shards(): other_half = lax.ppermute(sent, 'img', partners)  2.26 us
  transfers between devices with their start and end apart: 2, of which 2 were waited for; matrix products, arithmetic and copies ran while one was open for 0% of the time, Pallas kernels for 2%

profile of v3, /device:TPU:1, one launch (start us, length us, event | category | flops | bytes accessed | tf_op | source)
XLA Modules:
  0.0 58.1 jit_solution(2200367585116531020)
XLA Ops:
  0.6 3.6 %score.1 = (bf16[1184,256]{1,0:T(8,128)(2,1)S(1)}, bf16[1184,256]{1,0:T(8,128)(2,1)S(1)}, f32[64,2,128]{2,1,0:T(2,128)}) custom-call(f32[1,128]{1,0:T(1,128)} %bitcast.7, s32[1,128]{1,0:T(1,128)} %bitcast.8, bf16[128,4096]{1,0:T(8,128)(2,1)} %far_pixels.1, bf16[80,4096]{1,0:T(8,128)(2,1)} %far_proj.1, f32[1,4096]{1,0:T(1,128)} %bitcast.6, s32[1,128]{1,0:T(1,128)} %bitcast.9), custom_call_target="tpu_custom_call" | custom-call | tf_op jit(solution)/shard_map/score/pallas_call | solution.py:277
  4.3 14.9 %all-to-all-start = ((f32[64,2,128]{2,1,0:T(2,128)}), f32[64,2,128]{2,1,0:T(2,128)S(1)}, u32[]{:S(2)}, u32[]{:S(2)}) async-start(f32[64,2,128]{2,1,0:T(2,128)} %get-tuple-element.11), calls=%async_computation | async-start | bytes 131072 | tf_op jit(solution)/shard_map/all_to_all | solution.py:297
  19.2 2.3 %collective-permute-start = (bf16[1184,256]{1,0:T(8,128)(2,1)S(1)}, bf16[1184,256]{1,0:T(8,128)(2,1)S(1)}, u32[]{:S(2)}, u32[]{:S(2)}) collective-permute-start(bf16[1184,256]{1,0:T(8,128)(2,1)S(1)} %get-tuple-element.10), channel_id=1, source_target_pairs={{0,32},{32,0},{64,96},{96,64},{128,160},{160,128},{192,224},{224,1... | collective-permute-start | bytes 1818632 | tf_op jit(solution)/shard_map/ppermute | solution.py:310
  21.5 0.8 %own_terms.1 = (bf16[8,2,128,256]{3,2,1,0:T(8,128)(2,1)S(1)}, f32[4,16,128]{2,1,0:T(8,128)S(1)}) custom-call(bf16[1184,256]{1,0:T(8,128)(2,1)S(1)} %get-tuple-element.9.half, s32[1,64]{1,0:T(1,128)} %bitcast.10), custom_call_target="tpu_custom_call" | custom-call | flops 10000000000 | bytes 1572864 | tf_op jit(solution)/shard_map/own_terms/pallas_call | solution.py:300
  22.3 0.8 %collective-permute-done.half.other_half = bf16[1184,256]{1,0:T(8,128)(2,1)S(1)} collective-permute-done((bf16[1184,256]{1,0:T(8,128)(2,1)S(1)}, bf16[1184,256]{1,0:T(8,128)(2,1)S(1)}, u32[]{:S(2)}, u32[]{:S(2)}) %collective-permute-start) | collective-permute-done | bytes 606240 | tf_op jit(solution)/shard_map/ppermute | solution.py:310
  23.1 0.6 %other_terms.1.other_back = bf16[8,2,128,256]{3,2,1,0:T(8,128)(2,1)S(1)} custom-call(bf16[1184,256]{1,0:T(8,128)(2,1)S(1)} %collective-permute-done.half.other_half), custom_call_target="tpu_custom_call" | custom-call | flops 1 | bytes 1 | tf_op jit(solution)/shard_map/other_terms/pallas_call | solution.py:311
  23.8 5.0 %all-to-all-done.stats = f32[64,2,128]{2,1,0:T(2,128)S(1)} async-done(((f32[64,2,128]{2,1,0:T(2,128)}), f32[64,2,128]{2,1,0:T(2,128)S(1)}, u32[]{:S(2)}, u32[]{:S(2)}) %all-to-all-start) | async-done | bytes 65568 | tf_op jit(solution)/shard_map/all_to_all | solution.py:297
  28.8 0.6 back.1
  29.4 28.0 %all_to_all.10.parts = bf16[8,168,256]{2,1,0:T(8,128)(2,1)S(1)} all-to-all(bf16[8,168,256]{2,1,0:T(8,128)(2,1)S(1)} %back.1), channel_id=1, replica_groups={{0,64,128,192,256,320,384,448},{32,96,160,224,288,352,416,480},{1,65,12..., dimensions={0} | all-to-all | bytes 1376256 | tf_op jit(solution)/shard_map/all_to_all | solution.py:330
  57.4 0.7 %last.1 = (bf16[80,256]{1,0:T(8,128)(2,1)}, f32[1,128]{1,0:T(1,128)}) custom-call(bf16[8,168,256]{2,1,0:T(8,128)(2,1)S(1)} %all_to_all.10.parts, f32[4,16,128]{2,1,0:T(8,128)S(1)} %get-tuple-element.13.chosen), custom_call_target="tpu_custom_call" | custom-call | tf_op jit(solution)/shard_map/last/pallas_call | solution.py:331
Async XLA Ops:
  4.3 24.5 %all-to-all-start = ((f32[64,2,128]{2,1,0:T(2,128)}), f32[64,2,128]{2,1,0:T(2,128)S(1)}, u32[]{:S(2)}, u32[]{:S(2)}) async-start(f32[64,2,128]{2,1,0:T(2,128)} %get-tuple-element.11), calls=%async_computation | async-start | bytes 131072 | tf_op jit(solution)/shard_map/all_to_all | solution.py:297
  19.2 3.9 %collective-permute-start = (bf16[1184,256]{1,0:T(8,128)(2,1)S(1)}, bf16[1184,256]{1,0:T(8,128)(2,1)S(1)}, u32[]{:S(2)}, u32[]{:S(2)}) collective-permute-start(bf16[1184,256]{1,0:T(8,128)(2,1)S(1)} %get-tuple-element.10), channel_id=1, source_target_pairs={{0,32},{32,0},{64,96},{96,64},{128,160},{160,128},{192,224},{224,1... | collective-permute-start | bytes 1818632 | tf_op jit(solution)/shard_map/ppermute | solution.py:310

commit v4 on v3

--- a/solution.py
+++ b/solution.py
@@ -72,8 +72,8 @@
 
 
 def score_kernel(
-    far_defocus, far_limits, far_pixels, far_proj, far_noise, far_counts, kept, sent, stats,
-    defocus, limits, pixels, proj, noise, counts, terms, terms_sq, turn, edge, arrived,
+    far_defocus, far_limits, far_pixels, far_proj, far_noise, far_counts, kept, sent, far_stats,
+    defocus, limits, pixels, proj, noise, counts, terms, terms_sq, stats, turn, edge, arrived, left,
 ):
     rows, images = proj.shape[0], pixels.shape[0]
     copies = [
@@ -119,6 +119,8 @@
     mass = jnp.sum(jnp.where(significant, jnp.exp(found - peak), 0.0), axis=0, keepdims=True)
     both = jnp.concatenate([peak, mass], axis=0)
     stats[...] = jnp.broadcast_to(both[None], stats.shape)
+    leaving = pltpu.make_async_copy(stats, far_stats, left)
+    leaving.start()
     line = lax.broadcasted_iota(jnp.int32, (rows, images), 0)
     scalars = jnp.zeros((rows, images), F32)
     for k, part in enumerate((*thirds(defocus[...]), *thirds(limits[...].astype(F32)))):
@@ -135,6 +137,7 @@
         out[tail : tail + rows, LANES:] = second
         out[tail + rows :, :LANES] = third
         out[tail + rows :, LANES:] = scalars.astype(BF)
+    leaving.wait()
 
 
 def scores_of(half, rows):
@@ -204,7 +207,7 @@
 
 
 def back_kernel(half, other_half, stats, back, other_back, out):
-    rows = (out.shape[1] - PAD) // 2
+    rows = (out.shape[1] - PAD) // 4
     peers = stats.shape[0] // 2
     core = lax.rem(lax.axis_index("img"), 2)
     known = [evidence_of(stats[c * peers : (c + 1) * peers]) for c in range(2)]
@@ -215,35 +218,37 @@
 
     posterior = posterior_of(scores_of(half, rows), mine)
     other_posterior = posterior_of(scores_of(other_half, rows), other)
-    line = lax.broadcasted_iota(jnp.int32, (PAD, COLS), 0)
-    note = jnp.zeros((PAD, COLS), F32)
-    for k, part in enumerate(thirds(jnp.concatenate(known, axis=1))):
-        note = jnp.where(line == k, part.astype(F32), note)
+    line = lax.broadcasted_iota(jnp.int32, (PAD, LANES), 0)
+    note = jnp.zeros((PAD, LANES), F32)
+    for c in range(2):
+        for k, part in enumerate(thirds(known[c])):
+            note = jnp.where(line == 2 * k + c, part.astype(F32), note)
     note = note.astype(BF)
     for y in range(out.shape[0]):
         for k in range(2):
             part = jnp.dot(posterior, back[y, k], preferred_element_type=F32)
             part += jnp.dot(other_posterior, other_back[y, k], preferred_element_type=F32)
-            out[y, k * rows : (k + 1) * rows, :] = part.astype(BF)
-        out[y, 2 * rows :, :] = note
+            part = part.astype(BF)
+            out[y, 2 * k * rows : (2 * k + 1) * rows, :] = part[:, :LANES]
+            out[y, (2 * k + 1) * rows : (2 * k + 2) * rows, :] = part[:, LANES:]
+        out[y, 4 * rows :, :] = note
 
 
 def last_kernel(parts, chosen, far_reconstruction, far_evidence, reconstruction, evidence, sent):
     rows = reconstruction.shape[0]
     chips = parts.shape[0]
-    images = parts[0, :rows, :].astype(F32)
-    weights = parts[0, rows : 2 * rows, :].astype(F32)
-    for y in range(1, chips):
-        images += parts[y, :rows, :].astype(F32)
-        weights += parts[y, rows : 2 * rows, :].astype(F32)
-    reconstruction[...] = (images / (weights + 1.0)).astype(BF)
+    for h in range(2):
+        images, weights = (
+            sum(parts[y, (2 * k + h) * rows : (2 * k + h + 1) * rows, :].astype(F32) for y in range(chips))
+            for k in range(2)
+        )
+        reconstruction[:, h * LANES : (h + 1) * LANES] = (images / (weights + 1.0)).astype(BF)
     first = pltpu.make_async_copy(reconstruction, far_reconstruction, sent.at[0])
     first.start()
     lines = []
     for y in range(chips):
-        note = parts[y, 2 * rows :, :].astype(F32)
-        full = (note[0:1] + note[1:2]) + note[2:3]
-        lines += [full[:, :LANES], full[:, LANES:]]
+        note = parts[y, 4 * rows :, :].astype(F32)
+        lines += [(note[c : c + 1] + note[c + 2 : c + 3]) + note[c + 4 : c + 5] for c in range(2)]
     known = jnp.concatenate(lines, axis=0)
     placed = jnp.zeros((1, LANES), F32)
     for k in range(LANES // BLOCK):
@@ -283,13 +288,15 @@
             jax.ShapeDtypeStruct((2 * peers, 2, count), F32),
         ),
         in_specs=[pl.BlockSpec(memory_space=pltpu.HBM)] * 6,
-        out_specs=tuple(vmem(3)),
+        out_specs=(*vmem(2), pl.BlockSpec(memory_space=pltpu.HBM)),
         scratch_shapes=[
             *(pltpu.VMEM(a.shape, a.dtype) for a in operands),
             pltpu.VMEM((count, F), BF),
             pltpu.VMEM((count, F), BF),
+            pltpu.VMEM((2 * peers, 2, count), F32),
             *tables,
             pltpu.SemaphoreType.DMA((6,)),
+            pltpu.SemaphoreType.DMA,
         ],
         compiler_params=limit,
     )(*map(kept_far, operands))
@@ -321,7 +328,7 @@
     both = pl.pallas_call(
         back_kernel,
         name="back",
-        out_shape=jax.ShapeDtypeStruct((chips, 2 * rows + PAD, COLS), BF),
+        out_shape=jax.ShapeDtypeStruct((chips, 4 * rows + PAD, LANES), BF),
         in_specs=vmem(5),
         out_specs=vmem(1)[0],
         compiler_params=limit,

time: 58.4 us -> 58 us (level)
  transfers between devices with their start and end apart: 2 -> 2, of which waited for: 2 -> 2; matrix products, arithmetic and copies ran while one was open for 0% -> 0% of each run, Pallas kernels for 2% -> 3%
where the time goes in v4:
time: 58 us; the launch traced here: 57.8 us
  blocking collectives  27.7 us (48%)
  starting transfers between devices  17.2 us (30%)
  Pallas kernels  6.38 us (11%)
  waiting for transfers between devices  5.84 us (10%)
  between operations  0.68 us (1%)
    all_to_all x1, blocking collectives, shards(): lax.all_to_all(both, 'img', 0, 0, tiled=True, axis_index_groups=same_core)  27.7 us
    all_to_all x1, starting transfers between devices, shards(): lax.all_to_all(stats, ('img', 'proj'), 0, 0, tiled=True, axis_index_group...  14.9 us
    all_to_all x1, waiting for transfers between devices, shards(): lax.all_to_all(stats, ('img', 'proj'), 0, 0, tiled=True, axis_index_group...  5.04 us
    pallas_call x1, Pallas kernels, shards(): pl.pallas_call(score_kernel, name='score', out_shape=(shape, shape, jax.S...  3.63 us
    ppermute x1, starting transfers between devices, shards(): other_half = lax.ppermute(sent, 'img', partners)  2.26 us
  transfers between devices with their start and end apart: 2, of which 2 were waited for; matrix products, arithmetic and copies ran while one was open for 0% of the time, Pallas kernels for 3%

profile of v4, /device:TPU:1, one launch (start us, length us, event | category | flops | bytes accessed | tf_op | source)
XLA Modules:
  0.0 57.8 jit_solution(2401545121325389582)
XLA Ops:
  0.6 3.6 %score.1 = (bf16[1184,256]{1,0:T(8,128)(2,1)S(1)}, bf16[1184,256]{1,0:T(8,128)(2,1)S(1)}, f32[64,2,128]{2,1,0:T(2,128)}) custom-call(f32[1,128]{1,0:T(1,128)} %bitcast.7, s32[1,128]{1,0:T(1,128)} %bitcast.8, bf16[128,4096]{1,0:T(8,128)(2,1)} %far_pixels.1, bf16[80,4096]{1,0:T(8,128)(2,1)} %far_proj.1, f32[1,4096]{1,0:T(1,128)} %bitcast.6, s32[1,128]{1,0:T(1,128)} %bitcast.9), custom_call_target="tpu_custom_call" | custom-call | tf_op jit(solution)/shard_map/score/pallas_call | solution.py:282
  4.3 14.9 %all-to-all-start = ((f32[64,2,128]{2,1,0:T(2,128)}), f32[64,2,128]{2,1,0:T(2,128)S(1)}, u32[]{:S(2)}, u32[]{:S(2)}) async-start(f32[64,2,128]{2,1,0:T(2,128)} %get-tuple-element.11), calls=%async_computation | async-start | bytes 131072 | tf_op jit(solution)/shard_map/all_to_all | solution.py:304
  19.2 2.3 %collective-permute-start = (bf16[1184,256]{1,0:T(8,128)(2,1)S(1)}, bf16[1184,256]{1,0:T(8,128)(2,1)S(1)}, u32[]{:S(2)}, u32[]{:S(2)}) collective-permute-start(bf16[1184,256]{1,0:T(8,128)(2,1)S(1)} %get-tuple-element.10), channel_id=1, source_target_pairs={{0,32},{32,0},{64,96},{96,64},{128,160},{160,128},{192,224},{224,1... | collective-permute-start | bytes 1818632 | tf_op jit(solution)/shard_map/ppermute | solution.py:317
  21.5 0.8 %own_terms.1 = (bf16[8,2,128,256]{3,2,1,0:T(8,128)(2,1)S(1)}, f32[4,16,128]{2,1,0:T(8,128)S(1)}) custom-call(bf16[1184,256]{1,0:T(8,128)(2,1)S(1)} %get-tuple-element.9.half, s32[1,64]{1,0:T(1,128)} %bitcast.10), custom_call_target="tpu_custom_call" | custom-call | flops 10000000000 | bytes 1572864 | tf_op jit(solution)/shard_map/own_terms/pallas_call | solution.py:307
  22.3 0.8 %collective-permute-done.half.other_half = bf16[1184,256]{1,0:T(8,128)(2,1)S(1)} collective-permute-done((bf16[1184,256]{1,0:T(8,128)(2,1)S(1)}, bf16[1184,256]{1,0:T(8,128)(2,1)S(1)}, u32[]{:S(2)}, u32[]{:S(2)}) %collective-permute-start) | collective-permute-done | bytes 606240 | tf_op jit(solution)/shard_map/ppermute | solution.py:317
  23.2 0.6 %other_terms.1.other_back = bf16[8,2,128,256]{3,2,1,0:T(8,128)(2,1)S(1)} custom-call(bf16[1184,256]{1,0:T(8,128)(2,1)S(1)} %collective-permute-done.half.other_half), custom_call_target="tpu_custom_call" | custom-call | flops 1 | bytes 1 | tf_op jit(solution)/shard_map/other_terms/pallas_call | solution.py:318
  23.8 5.0 %all-to-all-done.stats = f32[64,2,128]{2,1,0:T(2,128)S(1)} async-done(((f32[64,2,128]{2,1,0:T(2,128)}), f32[64,2,128]{2,1,0:T(2,128)S(1)}, u32[]{:S(2)}, u32[]{:S(2)}) %all-to-all-start) | async-done | bytes 65568 | tf_op jit(solution)/shard_map/all_to_all | solution.py:304
  28.8 0.6 back.1
  29.4 27.7 %all_to_all.10.parts = bf16[8,328,128]{2,1,0:T(8,128)(2,1)S(1)} all-to-all(bf16[8,328,128]{2,1,0:T(8,128)(2,1)S(1)} %back.1), channel_id=1, replica_groups={{0,64,128,192,256,320,384,448},{32,96,160,224,288,352,416,480},{1,65,12..., dimensions={0} | all-to-all | bytes 1343488 | tf_op jit(solution)/shard_map/all_to_all | solution.py:337
  57.0 0.7 %last.1 = (bf16[80,256]{1,0:T(8,128)(2,1)}, f32[1,128]{1,0:T(1,128)}) custom-call(bf16[8,328,128]{2,1,0:T(8,128)(2,1)S(1)} %all_to_all.10.parts, f32[4,16,128]{2,1,0:T(8,128)S(1)} %get-tuple-element.13.chosen), custom_call_target="tpu_custom_call" | custom-call | tf_op jit(solution)/shard_map/last/pallas_call | solution.py:338
Async XLA Ops:
  4.3 24.5 %all-to-all-start = ((f32[64,2,128]{2,1,0:T(2,128)}), f32[64,2,128]{2,1,0:T(2,128)S(1)}, u32[]{:S(2)}, u32[]{:S(2)}) async-start(f32[64,2,128]{2,1,0:T(2,128)} %get-tuple-element.11), calls=%async_computation | async-start | bytes 131072 | tf_op jit(solution)/shard_map/all_to_all | solution.py:304
  19.2 3.9 %collective-permute-start = (bf16[1184,256]{1,0:T(8,128)(2,1)S(1)}, bf16[1184,256]{1,0:T(8,128)(2,1)S(1)}, u32[]{:S(2)}, u32[]{:S(2)}) collective-permute-start(bf16[1184,256]{1,0:T(8,128)(2,1)S(1)} %get-tuple-element.10), channel_id=1, source_target_pairs={{0,32},{32,0},{64,96},{96,64},{128,160},{160,128},{192,224},{224,1... | collective-permute-start | bytes 1818632 | tf_op jit(solution)/shard_map/ppermute | solution.py:317

commit v5 on v4

--- a/solution.py
+++ b/solution.py
@@ -117,8 +117,8 @@
     found = jnp.where(significant, total, NONE)
     peak = jnp.max(found, axis=0, keepdims=True)
     mass = jnp.sum(jnp.where(significant, jnp.exp(found - peak), 0.0), axis=0, keepdims=True)
-    both = jnp.concatenate([peak, mass], axis=0)
-    stats[...] = jnp.broadcast_to(both[None], stats.shape)
+    local = jnp.where(mass > 0.0, peak + jnp.log(mass), NONE)
+    stats[...] = jnp.broadcast_to(local[None], stats.shape)
     leaving = pltpu.make_async_copy(stats, far_stats, left)
     leaving.start()
     line = lax.broadcasted_iota(jnp.int32, (rows, images), 0)
@@ -200,10 +200,9 @@
 
 
 def evidence_of(stats):
-    peaks, masses = stats[:, 0, :], stats[:, 1, :]
-    peak = jnp.max(peaks, axis=0, keepdims=True)
-    mass = jnp.sum(masses * jnp.exp(peaks - peak), axis=0, keepdims=True)
-    return peak + jnp.log(mass)
+    local = stats[:, 0, :]
+    peak = jnp.max(local, axis=0, keepdims=True)
+    return peak + jnp.log(jnp.sum(jnp.exp(local - peak), axis=0, keepdims=True))
 
 
 def back_kernel(half, other_half, stats, back, other_back, out):
@@ -285,7 +284,7 @@
         out_shape=(
             shape,
             shape,
-            jax.ShapeDtypeStruct((2 * peers, 2, count), F32),
+            jax.ShapeDtypeStruct((2 * peers, 1, count), F32),
         ),
         in_specs=[pl.BlockSpec(memory_space=pltpu.HBM)] * 6,
         out_specs=(*vmem(2), pl.BlockSpec(memory_space=pltpu.HBM)),
@@ -293,7 +292,7 @@
             *(pltpu.VMEM(a.shape, a.dtype) for a in operands),
             pltpu.VMEM((count, F), BF),
             pltpu.VMEM((count, F), BF),
-            pltpu.VMEM((2 * peers, 2, count), F32),
+            pltpu.VMEM((2 * peers, 1, count), F32),
             *tables,
             pltpu.SemaphoreType.DMA((6,)),
             pltpu.SemaphoreType.DMA,

time: 58 us -> 55.8 us (0.962)
  blocking collectives: 27.7 us -> 26 us
    all_to_all x1, blocking collectives: 27.7 us -> 26 us  [shards(): lax.all_to_all(both, 'img', 0, 0, tiled=True, axis_index_groups=same_core)]
where the time goes in v5:
time: 55.8 us; the launch traced here: 55.5 us
  blocking collectives  26 us (47%)
  starting transfers between devices  17.2 us (31%)
  Pallas kernels  6.39 us (11%)
  waiting for transfers between devices  5.29 us (9%)
  between operations  0.68 us (1%)
    all_to_all x1, blocking collectives, shards(): lax.all_to_all(both, 'img', 0, 0, tiled=True, axis_index_groups=same_core)  26 us
    all_to_all x1, starting transfers between devices, shards(): lax.all_to_all(stats, ('img', 'proj'), 0, 0, tiled=True, axis_index_group...  14.9 us
    all_to_all x1, waiting for transfers between devices, shards(): lax.all_to_all(stats, ('img', 'proj'), 0, 0, tiled=True, axis_index_group...  4.49 us
    pallas_call x1, Pallas kernels, shards(): pl.pallas_call(score_kernel, name='score', out_shape=(shape, shape, jax.S...  3.64 us
    ppermute x1, starting transfers between devices, shards(): other_half = lax.ppermute(sent, 'img', partners)  2.26 us
  transfers between devices with their start and end apart: 2, of which 2 were waited for; matrix products, arithmetic and copies ran while one was open for 0% of the time, Pallas kernels for 3%

profile of v5, /device:TPU:1, one launch (start us, length us, event | category | flops | bytes accessed | tf_op | source)
XLA Modules:
  0.0 55.5 jit_solution(8756636086816230607)
XLA Ops:
  0.6 3.6 %score.1 = (bf16[1184,256]{1,0:T(8,128)(2,1)S(1)}, bf16[1184,256]{1,0:T(8,128)(2,1)S(1)}, f32[64,1,128]{2,1,0:T(1,128)}) custom-call(f32[1,128]{1,0:T(1,128)} %bitcast.7, s32[1,128]{1,0:T(1,128)} %bitcast.8, bf16[128,4096]{1,0:T(8,128)(2,1)} %far_pixels.1, bf16[80,4096]{1,0:T(8,128)(2,1)} %far_proj.1, f32[1,4096]{1,0:T(1,128)} %bitcast.6, s32[1,128]{1,0:T(1,128)} %bitcast.9), custom_call_target="tpu_custom_call" | custom-call | tf_op jit(solution)/shard_map/score/pallas_call | solution.py:281
  4.3 14.9 %all-to-all-start = ((f32[64,1,128]{2,1,0:T(1,128)}), f32[64,1,128]{2,1,0:T(1,128)S(1)}, u32[]{:S(2)}, u32[]{:S(2)}) async-start(f32[64,1,128]{2,1,0:T(1,128)} %get-tuple-element.11), calls=%async_computation | async-start | bytes 65536 | tf_op jit(solution)/shard_map/all_to_all | solution.py:303
  19.2 2.3 %collective-permute-start = (bf16[1184,256]{1,0:T(8,128)(2,1)S(1)}, bf16[1184,256]{1,0:T(8,128)(2,1)S(1)}, u32[]{:S(2)}, u32[]{:S(2)}) collective-permute-start(bf16[1184,256]{1,0:T(8,128)(2,1)S(1)} %get-tuple-element.10), channel_id=1, source_target_pairs={{0,32},{32,0},{64,96},{96,64},{128,160},{160,128},{192,224},{224,1... | collective-permute-start | bytes 1818632 | tf_op jit(solution)/shard_map/ppermute | solution.py:316
  21.5 0.8 %own_terms.1 = (bf16[8,2,128,256]{3,2,1,0:T(8,128)(2,1)S(1)}, f32[4,16,128]{2,1,0:T(8,128)S(1)}) custom-call(bf16[1184,256]{1,0:T(8,128)(2,1)S(1)} %get-tuple-element.9.half, s32[1,64]{1,0:T(1,128)} %bitcast.10), custom_call_target="tpu_custom_call" | custom-call | flops 10000000000 | bytes 1572864 | tf_op jit(solution)/shard_map/own_terms/pallas_call | solution.py:306
  22.4 0.8 %collective-permute-done.half.other_half = bf16[1184,256]{1,0:T(8,128)(2,1)S(1)} collective-permute-done((bf16[1184,256]{1,0:T(8,128)(2,1)S(1)}, bf16[1184,256]{1,0:T(8,128)(2,1)S(1)}, u32[]{:S(2)}, u32[]{:S(2)}) %collective-permute-start) | collective-permute-done | bytes 606240 | tf_op jit(solution)/shard_map/ppermute | solution.py:316
  23.2 0.6 %other_terms.1.other_back = bf16[8,2,128,256]{3,2,1,0:T(8,128)(2,1)S(1)} custom-call(bf16[1184,256]{1,0:T(8,128)(2,1)S(1)} %collective-permute-done.half.other_half), custom_call_target="tpu_custom_call" | custom-call | flops 1 | bytes 1 | tf_op jit(solution)/shard_map/other_terms/pallas_call | solution.py:317
  23.8 4.5 %all-to-all-done.stats = f32[64,1,128]{2,1,0:T(1,128)S(1)} async-done(((f32[64,1,128]{2,1,0:T(1,128)}), f32[64,1,128]{2,1,0:T(1,128)S(1)}, u32[]{:S(2)}, u32[]{:S(2)}) %all-to-all-start) | async-done | bytes 32800 | tf_op jit(solution)/shard_map/all_to_all | solution.py:303
  28.3 0.6 %back.1 = bf16[8,328,128]{2,1,0:T(8,128)(2,1)S(1)} custom-call(bf16[1184,256]{1,0:T(8,128)(2,1)S(1)} %get-tuple-element.9.half, bf16[1184,256]{1,0:T(8,128)(2,1)S(1)} %collective-permute-done.half.other_half, f32[64,1,128]{2,1,0:T(1,128)S(1)} %all-to-all-done.stats, bf16[8,2,128,256]{3,2,1,0:T(8,128)(2,1)S(1)} %get-tuple-element.12.back, ...), custom_call_target="tpu_custom_call" | custom-call | tf_op jit(solution)/shard_map/back/pallas_call | solution.py:327
  28.8 26.0 %all_to_all.10.parts = bf16[8,328,128]{2,1,0:T(8,128)(2,1)S(1)} all-to-all(bf16[8,328,128]{2,1,0:T(8,128)(2,1)S(1)} %back.1), channel_id=1, replica_groups={{0,64,128,192,256,320,384,448},{32,96,160,224,288,352,416,480},{1,65,12..., dimensions={0} | all-to-all | bytes 1343488 | tf_op jit(solution)/shard_map/all_to_all | solution.py:336
  54.8 0.7 %last.1 = (bf16[80,256]{1,0:T(8,128)(2,1)}, f32[1,128]{1,0:T(1,128)}) custom-call(bf16[8,328,128]{2,1,0:T(8,128)(2,1)S(1)} %all_to_all.10.parts, f32[4,16,128]{2,1,0:T(8,128)S(1)} %get-tuple-element.13.chosen), custom_call_target="tpu_custom_call" | custom-call | tf_op jit(solution)/shard_map/last/pallas_call | solution.py:337
Async XLA Ops:
  4.3 24.0 %all-to-all-start = ((f32[64,1,128]{2,1,0:T(1,128)}), f32[64,1,128]{2,1,0:T(1,128)S(1)}, u32[]{:S(2)}, u32[]{:S(2)}) async-start(f32[64,1,128]{2,1,0:T(1,128)} %get-tuple-element.11), calls=%async_computation | async-start | bytes 65536 | tf_op jit(solution)/shard_map/all_to_all | solution.py:303
  19.2 3.9 %collective-permute-start = (bf16[1184,256]{1,0:T(8,128)(2,1)S(1)}, bf16[1184,256]{1,0:T(8,128)(2,1)S(1)}, u32[]{:S(2)}, u32[]{:S(2)}) collective-permute-start(bf16[1184,256]{1,0:T(8,128)(2,1)S(1)} %get-tuple-element.10), channel_id=1, source_target_pairs={{0,32},{32,0},{64,96},{96,64},{128,160},{160,128},{192,224},{224,1... | collective-permute-start | bytes 1818632 | tf_op jit(solution)/shard_map/ppermute | solution.py:316

commit v6 on v5

--- a/solution.py
+++ b/solution.py
@@ -215,8 +215,9 @@
     def posterior_of(scores, evidence):
         return jnp.where(scores > 0.5 * NONE, jnp.exp(scores - evidence), 0.0).astype(BF)
 
-    posterior = posterior_of(scores_of(half, rows), mine)
-    other_posterior = posterior_of(scores_of(other_half, rows), other)
+    posterior = jnp.concatenate(
+        [posterior_of(scores_of(half, rows), mine), posterior_of(scores_of(other_half, rows), other)], axis=1
+    )
     line = lax.broadcasted_iota(jnp.int32, (PAD, LANES), 0)
     note = jnp.zeros((PAD, LANES), F32)
     for c in range(2):
@@ -225,9 +226,8 @@
     note = note.astype(BF)
     for y in range(out.shape[0]):
         for k in range(2):
-            part = jnp.dot(posterior, back[y, k], preferred_element_type=F32)
-            part += jnp.dot(other_posterior, other_back[y, k], preferred_element_type=F32)
-            part = part.astype(BF)
+            terms = jnp.concatenate([back[y, k], other_back[y, k]], axis=0)
+            part = jnp.dot(posterior, terms, preferred_element_type=F32).astype(BF)
             out[y, 2 * k * rows : (2 * k + 1) * rows, :] = part[:, :LANES]
             out[y, (2 * k + 1) * rows : (2 * k + 2) * rows, :] = part[:, LANES:]
         out[y, 4 * rows :, :] = note

time: 55.8 us -> 55.8 us (level)
  no operation moved by 1% of the time
where the time goes in v6:
time: 55.8 us; the launch traced here: 55.5 us
  blocking collectives  26 us (47%)
  starting transfers between devices  17.2 us (31%)
  Pallas kernels  6.37 us (11%)
  waiting for transfers between devices  5.29 us (9%)
  between operations  0.67 us (1%)
    all_to_all x1, blocking collectives, shards(): lax.all_to_all(both, 'img', 0, 0, tiled=True, axis_index_groups=same_core)  26 us
    all_to_all x1, starting transfers between devices, shards(): lax.all_to_all(stats, ('img', 'proj'), 0, 0, tiled=True, axis_index_group...  14.9 us
    all_to_all x1, waiting for transfers between devices, shards(): lax.all_to_all(stats, ('img', 'proj'), 0, 0, tiled=True, axis_index_group...  4.49 us
    pallas_call x1, Pallas kernels, shards(): pl.pallas_call(score_kernel, name='score', out_shape=(shape, shape, jax.S...  3.64 us
    ppermute x1, starting transfers between devices, shards(): other_half = lax.ppermute(sent, 'img', partners)  2.26 us
  transfers between devices with their start and end apart: 2, of which 2 were waited for; matrix products, arithmetic and copies ran while one was open for 0% of the time, Pallas kernels for 3%

profile of v6, /device:TPU:1, one launch (start us, length us, event | category | flops | bytes accessed | tf_op | source)
XLA Modules:
  0.0 55.5 jit_solution(18096189683474862335)
XLA Ops:
  0.6 3.6 %score.1 = (bf16[1184,256]{1,0:T(8,128)(2,1)S(1)}, bf16[1184,256]{1,0:T(8,128)(2,1)S(1)}, f32[64,1,128]{2,1,0:T(1,128)}) custom-call(f32[1,128]{1,0:T(1,128)} %bitcast.7, s32[1,128]{1,0:T(1,128)} %bitcast.8, bf16[128,4096]{1,0:T(8,128)(2,1)} %far_pixels.1, bf16[80,4096]{1,0:T(8,128)(2,1)} %far_proj.1, f32[1,4096]{1,0:T(1,128)} %bitcast.6, s32[1,128]{1,0:T(1,128)} %bitcast.9), custom_call_target="tpu_custom_call" | custom-call | tf_op jit(solution)/shard_map/score/pallas_call | solution.py:281
  4.3 14.9 %all-to-all-start = ((f32[64,1,128]{2,1,0:T(1,128)}), f32[64,1,128]{2,1,0:T(1,128)S(1)}, u32[]{:S(2)}, u32[]{:S(2)}) async-start(f32[64,1,128]{2,1,0:T(1,128)} %get-tuple-element.11), calls=%async_computation | async-start | bytes 65536 | tf_op jit(solution)/shard_map/all_to_all | solution.py:303
  19.2 2.3 %collective-permute-start = (bf16[1184,256]{1,0:T(8,128)(2,1)S(1)}, bf16[1184,256]{1,0:T(8,128)(2,1)S(1)}, u32[]{:S(2)}, u32[]{:S(2)}) collective-permute-start(bf16[1184,256]{1,0:T(8,128)(2,1)S(1)} %get-tuple-element.10), channel_id=1, source_target_pairs={{0,32},{32,0},{64,96},{96,64},{128,160},{160,128},{192,224},{224,1... | collective-permute-start | bytes 1818632 | tf_op jit(solution)/shard_map/ppermute | solution.py:316
  21.5 0.8 %own_terms.1 = (bf16[8,2,128,256]{3,2,1,0:T(8,128)(2,1)S(1)}, f32[4,16,128]{2,1,0:T(8,128)S(1)}) custom-call(bf16[1184,256]{1,0:T(8,128)(2,1)S(1)} %get-tuple-element.9.half, s32[1,64]{1,0:T(1,128)} %bitcast.10), custom_call_target="tpu_custom_call" | custom-call | flops 10000000000 | bytes 1572864 | tf_op jit(solution)/shard_map/own_terms/pallas_call | solution.py:306
  22.4 0.8 %collective-permute-done.half.other_half = bf16[1184,256]{1,0:T(8,128)(2,1)S(1)} collective-permute-done((bf16[1184,256]{1,0:T(8,128)(2,1)S(1)}, bf16[1184,256]{1,0:T(8,128)(2,1)S(1)}, u32[]{:S(2)}, u32[]{:S(2)}) %collective-permute-start) | collective-permute-done | bytes 606240 | tf_op jit(solution)/shard_map/ppermute | solution.py:316
  23.2 0.6 %other_terms.1.other_back = bf16[8,2,128,256]{3,2,1,0:T(8,128)(2,1)S(1)} custom-call(bf16[1184,256]{1,0:T(8,128)(2,1)S(1)} %collective-permute-done.half.other_half), custom_call_target="tpu_custom_call" | custom-call | flops 1 | bytes 1 | tf_op jit(solution)/shard_map/other_terms/pallas_call | solution.py:317
  23.8 4.5 %all-to-all-done.stats = f32[64,1,128]{2,1,0:T(1,128)S(1)} async-done(((f32[64,1,128]{2,1,0:T(1,128)}), f32[64,1,128]{2,1,0:T(1,128)S(1)}, u32[]{:S(2)}, u32[]{:S(2)}) %all-to-all-start) | async-done | bytes 32800 | tf_op jit(solution)/shard_map/all_to_all | solution.py:303
  28.3 0.5 back.1
  28.8 26.0 %all_to_all.10.parts = bf16[8,328,128]{2,1,0:T(8,128)(2,1)S(1)} all-to-all(bf16[8,328,128]{2,1,0:T(8,128)(2,1)S(1)} %back.1), channel_id=1, replica_groups={{0,64,128,192,256,320,384,448},{32,96,160,224,288,352,416,480},{1,65,12..., dimensions={0} | all-to-all | bytes 1343488 | tf_op jit(solution)/shard_map/all_to_all | solution.py:336
  54.8 0.7 %last.1 = (bf16[80,256]{1,0:T(8,128)(2,1)}, f32[1,128]{1,0:T(1,128)}) custom-call(bf16[8,328,128]{2,1,0:T(8,128)(2,1)S(1)} %all_to_all.10.parts, f32[4,16,128]{2,1,0:T(8,128)S(1)} %get-tuple-element.13.chosen), custom_call_target="tpu_custom_call" | custom-call | tf_op jit(solution)/shard_map/last/pallas_call | solution.py:337
Async XLA Ops:
  4.3 24.0 %all-to-all-start = ((f32[64,1,128]{2,1,0:T(1,128)}), f32[64,1,128]{2,1,0:T(1,128)S(1)}, u32[]{:S(2)}, u32[]{:S(2)}) async-start(f32[64,1,128]{2,1,0:T(1,128)} %get-tuple-element.11), calls=%async_computation | async-start | bytes 65536 | tf_op jit(solution)/shard_map/all_to_all | solution.py:303
  19.2 3.9 %collective-permute-start = (bf16[1184,256]{1,0:T(8,128)(2,1)S(1)}, bf16[1184,256]{1,0:T(8,128)(2,1)S(1)}, u32[]{:S(2)}, u32[]{:S(2)}) collective-permute-start(bf16[1184,256]{1,0:T(8,128)(2,1)S(1)} %get-tuple-element.10), channel_id=1, source_target_pairs={{0,32},{32,0},{64,96},{96,64},{128,160},{160,128},{192,224},{224,1... | collective-permute-start | bytes 1818632 | tf_op jit(solution)/shard_map/ppermute | solution.py:316
